TPU v7x, 128 devices: a whole 4x4x4 slice. The times are simulated.
128 devices in a mesh: sub: 2 (over x_hi), dp: 16 (over z, y), mp: 4 (over x_lo, core).
Axes of the slice: x: 4 (x_hi: 2, x_lo: 2; x = x_hi * 2 + x_lo), y: 4, z: 4, core: 2. Of those that a mesh axis runs over, the one named last changes fastest.
Arguments:
- features: bfloat16 [16384, 1024], P(('sub', 'dp', 'mp')), may hold values from -6 to 6
- teacher: bfloat16 [16384, 1024], P(('sub', 'dp', 'mp')), may hold values from -6 to 6
- proj: bfloat16 [1024, 1024], replicated, may hold values from -0.1875 to 0.1875
Outputs:
- feature_grad: float32 [16384, 1024], P(('sub', 'dp', 'mp'))
All inputs are finite; a program needn't handle non-finite values.
Results may differ from a plain program's by a relative error of at most 0.0095.
Values may be sent and summed in bfloat16 or wider, within the bound.
A program may use at most 128 MiB of HBM per device.

v0:
```python
import jax
import jax.numpy as jnp
from jax import lax
from jax.sharding import PartitionSpec as P

logit_scale = 100.0
epsilon = 1e-06


def joined(value, axis, join):
    pieces = jax.tree.map(lambda part: lax.all_gather(part, axis), value)
    head = jax.tree.map(lambda part: part[0], pieces)
    tail = jax.tree.map(lambda part: part[1:], pieces)
    running, _ = lax.scan(lambda running, piece: (join(running, piece), None), head, tail)
    return running


def unit_rows(values):
    norm_rows = jnp.sqrt(jnp.sum(values * values, axis=1, keepdims=True) + epsilon)
    return (values / norm_rows, norm_rows)


def partial_totals(score, diagonal_mask):
    row_top = jnp.max(jnp.where(diagonal_mask, -jnp.inf, score), axis=1)
    row_sum = jnp.sum(jnp.where(diagonal_mask, 0.0, jnp.exp(score - row_top[:, None])), axis=1)
    return (row_top, row_sum)


def join_totals(top_first, sum_first, top_second, sum_second):
    larger = jnp.maximum(top_first, top_second)
    return (
        larger,
        sum_first * jnp.exp(top_first - larger) + sum_second * jnp.exp(top_second - larger),
    )


def combine_totals(first, second):
    s_top, s_sum = join_totals(first[0], first[1], second[0], second[1])
    t_top, t_sum = join_totals(first[2], first[3], second[2], second[3])
    return (s_top, s_sum, t_top, t_sum)


def per_device(features, teacher, proj):
    student = jnp.dot(features, proj, preferred_element_type=jnp.float32)
    student_unit, student_norm = unit_rows(student)
    own_student = student_unit.astype(jnp.bfloat16)
    own_teacher = unit_rows(teacher.astype(jnp.float32))[0].astype(jnp.bfloat16)
    width = own_student.shape[0]
    group_student, group_teacher = (
        lax.all_gather(own_student, "mp", axis=0, tiled=True),
        lax.all_gather(own_teacher, "mp", axis=0, tiled=True),
    )
    column_student, column_teacher = (
        lax.all_gather(own_student, ("sub", "dp"), axis=0, tiled=True),
        lax.all_gather(own_teacher, ("sub", "dp"), axis=0, tiled=True),
    )
    group_rows = group_student.shape[0]
    group = lax.axis_index(("sub", "dp"))
    member = lax.axis_index("mp")
    row_ids = group * group_rows + jnp.arange(group_rows, dtype=jnp.int32)[:, None]
    column_range = jnp.arange(column_student.shape[0], dtype=jnp.int32)
    column_ids = column_range // width * group_rows + member * width + column_range % width
    diagonal_mask = row_ids == column_ids[None, :]
    pair_dims = (((1,), (1,)), ((), ()))
    s_score = logit_scale * lax.dot_general(
        group_student, column_student, pair_dims, preferred_element_type=jnp.float32
    )
    t_score = logit_scale * lax.dot_general(
        group_teacher, column_teacher, pair_dims, preferred_element_type=jnp.float32
    )
    s_top, s_sum = partial_totals(s_score, diagonal_mask)
    t_top, t_sum = partial_totals(t_score, diagonal_mask)
    s_top, s_sum, t_top, t_sum = joined((s_top, s_sum, t_top, t_sum), "mp", combine_totals)
    values = (
        jnp.exp(s_score - s_top[:, None]) / s_sum[:, None]
        - jnp.exp(t_score - t_top[:, None]) / t_sum[:, None]
    )
    own_weight = jnp.where(diagonal_mask, 0.0, values).astype(jnp.bfloat16)
    weight_list = (own_weight,)
    weight = weight_list[0]
    result = jnp.dot(weight, column_student, preferred_element_type=jnp.float32)
    grad = lax.psum_scatter(result, "mp", scatter_dimension=0, tiled=True)
    grad = grad + lax.psum_scatter(
        lax.dot_general(
            own_weight, group_student, (((0,), (0,)), ((), ())), preferred_element_type=jnp.float32
        ),
        ("sub", "dp"),
        scatter_dimension=0,
        tiled=True,
    )
    grad = logit_scale * grad
    along = jnp.sum(student_unit * grad, axis=1, keepdims=True)
    d_student = ((grad - student_unit * along) / student_norm).astype(jnp.bfloat16)
    return lax.dot_general(d_student, proj, pair_dims, preferred_element_type=jnp.float32)


def solution(mesh):
    in_specs = (P(("sub", "dp", "mp"), None), P(("sub", "dp", "mp"), None), P())
    out_specs = P(("sub", "dp", "mp"), None)
    return jax.shard_map(
        per_device, mesh=mesh, in_specs=in_specs, out_specs=out_specs, check_vma=False
    )
```

profile of v0, /device:TPU:0, one launch (start us, length us, event | category | flops | bytes accessed | tf_op | source)
XLA Modules:
  0.0 596.0 jit_solution(2389917719710216734)
XLA Ops:
  6.5 1.6 copy-done
  8.1 1.5 multiply_reduce_fusion.1
  9.6 0.8 fusion.21
  11.3 1.1 fusion.5
  12.4 1.8 fusion.6
  14.8 18.9 %all-gather.13.cloned.1.call-done = bf16[512,1024]{1,0:T(8,128)(2,1)} async-done(((bf16[128,1024]{1,0:T(8,128)(2,1)}), bf16[512,1024]{1,0:T(8,128)(2,1)}) %all-gather.13.cloned.1.call-update) | async-done | bytes 1048592 | tf_op jit(solution)/shard_map/all_gather | solution.py:50
  33.7 107.9 %all-gather.15.cloned.1.call-done = bf16[4096,1024]{1,0:T(8,128)(2,1)} async-done(((bf16[128,1024]{1,0:T(8,128)(2,1)}), bf16[4096,1024]{1,0:T(8,128)(2,1)}) %all-gather.15.cloned.1.call-update) | async-done | bytes 8388624 | tf_op jit(solution)/shard_map/all_gather | solution.py:54
  141.7 11.5 %fusion.22 = f32[512,4096]{1,0:T(8,128)} fusion(bf16[512,1024]{1,0:T(8,128)(2,1)} %all-gather.13.cloned.1.call-done, bf16[4096,1024]{1,0:T(8,128)(2,1)} %all-gather.15.cloned.1.call-done), kind=kOutput, calls=%fused_computation.51 | convolution fusion | flops 4294967296 | bytes 17825792 | tf_op jit(solution)/shard_map/dot_general | solution.py:65
  153.1 8.8 %all-gather.17.cloned.1.call-done = bf16[512,1024]{1,0:T(8,128)(2,1)} async-done(((bf16[128,1024]{1,0:T(8,128)(2,1)}), bf16[512,1024]{1,0:T(8,128)(2,1)}) %all-gather.17.cloned.1.call-update) | async-done | bytes 1048592 | tf_op jit(solution)/shard_map/all_gather | solution.py:51
  162.0 107.8 %all-gather.19.cloned.1.call-done = bf16[4096,1024]{1,0:T(8,128)(2,1)} async-done(((bf16[128,1024]{1,0:T(8,128)(2,1)}), bf16[4096,1024]{1,0:T(8,128)(2,1)}) %all-gather.19.cloned.1.call-update) | async-done | bytes 8388624 | tf_op jit(solution)/shard_map/all_gather | solution.py:55
  269.7 14.8 %fusion.2 = (f32[512]{0:T(512)S(1)}, f32[512]{0:T(512)S(1)}, f32[512,4096]{1,0:T(8,128)}) fusion(s32[4096]{0:T(1024)S(1)} %fusion.18, s32[512]{0:T(512)S(1)} %iota_add_fusion, f32[512,4096]{1,0:T(8,128)} %fusion.22, bf16[512,1024]{1,0:T(8,128)(2,1)} %all-gather.17.cloned.1.call-done, bf16[4096,1024]{1,0:T(8,128)(2,1)} %all-gather.19.cloned.1.call-done), kind=kOutput, calls=%fused_computation.13 | convolution fusion | flops 4309646336 | bytes 26236928 | tf_op jit(solution)/shard_map/dot_general | solution.py:68
  284.6 6.3 %fusion.3 = (f32[512]{0:T(512)S(1)}, f32[512]{0:T(512)S(1)}) fusion(f32[512,4096]{1,0:T(8,128)} %get-tuple-element.89, f32[512]{0:T(512)S(1)} %get-tuple-element.61, s32[4096]{0:T(1024)S(1)} %fusion.18, s32[512]{0:T(512)S(1)} %iota_add_fusion, f32[512]{0:T(512)S(1)} %get-tuple-element.62, f32[512,4096]{1,0:T(8,128)S(1)} %copy-done.1), kind=kLoop, calls=%fused_computation.14 | loop fusion | flops 18873344 | bytes 16803840 | tf_op jit(solution)/shard_map/reduce_sum | solution.py:25
  290.9 5.3 all-gather.7
  296.2 5.1 all-gather.5
  301.4 5.1 all-gather.4
  306.5 5.1 all-gather.6
  312.0 8.4 %fusion.4 = bf16[512,4096]{1,0:T(8,128)(2,1)S(1)} fusion(f32[512,4096]{1,0:T(8,128)} %get-tuple-element.89, f32[512,4096]{1,0:T(8,128)} %fusion.22, f32[512]{0:T(512)S(1)} %get-tuple-element.58, f32[512]{0:T(512)S(1)} %get-tuple-element.57, f32[512]{0:T(512)S(1)} %get-tuple-element.56, f32[512]{0:T(512)S(1)} %get-tuple-element.55, s32[4096]{0:T(1024)S(1)} %fusion.18, ...), kind=kLoop, calls=%fused_computation.15 | loop fusion | flops 20971520 | bytes 20998144 | tf_op jit(solution)/shard_map/convert_element_type | solution.py:78
  320.5 1.9 copy-done.2
  322.4 8.3 %fusion.23 = f32[512,1024]{1,0:T(8,128)} fusion(bf16[512,4096]{1,0:T(8,128)(2,1)S(1)} %fusion.4, bf16[4096,1024]{1,0:T(8,128)(2,1)} %all-gather.15.cloned.1.call-done), kind=kOutput, calls=%fused_computation.52 | convolution fusion | flops 4294967296 | bytes 14680064 | tf_op jit(solution)/shard_map/dot_general | solution.py:81
  330.7 12.8 %fusion.24 = f32[4096,1024]{1,0:T(8,128)} fusion(bf16[512,4096]{1,0:T(8,128)(2,1)} %copy-done.2, bf16[512,1024]{1,0:T(8,128)(2,1)} %all-gather.13.cloned.1.call-done), kind=kOutput, calls=%fused_computation.53 | convolution fusion | flops 4294967296 | bytes 22020096 | tf_op jit(solution)/shard_map/dot_general | solution.py:84
  343.5 13.4 %reduce-scatter.3.cloned.1.call-done = f32[128,1024]{1,0:T(8,128)} async-done(((f32[512,1024]{1,0:T(8,128)}), f32[128,1024]{1,0:T(8,128)}) %reduce-scatter.3.cloned.1.call-update) | async-done | bytes 524304 | tf_op jit(solution)/shard_map/reduce_scatter | solution.py:82
  356.9 228.0 %reduce-scatter.5.cloned.1.call-done = f32[128,1024]{1,0:T(8,128)} async-done(((f32[4096,1024]{1,0:T(8,128)}), f32[128,1024]{1,0:T(8,128)}) %reduce-scatter.5.cloned.1.call-update) | async-done | bytes 524304 | tf_op jit(solution)/shard_map/reduce_scatter | solution.py:83
  584.9 1.4 multiply_reduce_fusion
  586.3 2.8 fusion.7
  (48 shorter events, 2.1 us)
Async XLA Ops:
  6.5 1.6 copy-start
  6.5 27.2 %all-gather.13.cloned.1.call-start = ((), (), s32[]{:S(2)}) async-start(), calls=%async_computation.2 | async-start | bytes 1310720 | tf_op jit(solution)/shard_map/all_gather | solution.py:50
  10.5 131.2 %all-gather.15.cloned.1.call-start = ((), (), s32[]{:S(2)}) async-start(), calls=%async_computation.3 | async-start | bytes 8650752 | tf_op jit(solution)/shard_map/all_gather | solution.py:54
  11.2 150.7 %all-gather.17.cloned.1.call-start = ((), (), s32[]{:S(2)}) async-start(), calls=%async_computation.4 | async-start | bytes 1310720 | tf_op jit(solution)/shard_map/all_gather | solution.py:51
  14.2 255.6 %all-gather.19.cloned.1.call-start = ((), (), s32[]{:S(2)}) async-start(), calls=%async_computation.5 | async-start | bytes 8650752 | tf_op jit(solution)/shard_map/all_gather | solution.py:55
  14.7 342.2 %reduce-scatter.3.cloned.1.call-start = ((), (), s32[]{:S(2)}) async-start(), calls=%async_computation.6 | async-start | bytes 2621440 | tf_op jit(solution)/shard_map/reduce_scatter | solution.py:82
  269.7 14.8 %copy-start.1 = (f32[512,4096]{1,0:T(8,128)S(1)}, f32[512,4096]{1,0:T(8,128)}, u32[]{:S(2)}) copy-start(f32[512,4096]{1,0:T(8,128)} %fusion.22) | copy-start | bytes 25165828
  320.4 1.9 copy-start.2
  330.7 254.3 %reduce-scatter.5.cloned.1.call-start = ((), (), s32[]{:S(2)}) async-start(), calls=%async_computation.7 | async-start | bytes 17301504 | tf_op jit(solution)/shard_map/reduce_scatter | solution.py:83
Sparse Core Ops, SparseCore 0:
  10.6 23.1 all-gather.12
  36.8 104.7 all-gather.14
  143.3 18.5 all-gather.16
  164.9 104.7 all-gather.18
  330.8 26.1 reduce-scatter.2
  359.3 225.5 reduce-scatter.4
where the time goes:
time: 596 us
  waiting for transfers between devices  486 us (82%)
  matrix products  51.7 us (9%)
  blocking collectives  20.8 us (3%)
  other arithmetic  19.9 us (3%)
  between operations  13.6 us (2%)
    reduce_scatter x1, waiting for transfers between devices, per_device(): lax.psum_scatter(lax.dot_general(own_weight, group_student, (((0,), (0,))...  228 us
    all_gather x1, waiting for transfers between devices, per_device(): lax.all_gather(own_student, ('sub', 'dp'), axis=0, tiled=True)  108 us
    all_gather x1, waiting for transfers between devices, per_device(): lax.all_gather(own_teacher, ('sub', 'dp'), axis=0, tiled=True)  108 us
    all_gather x4, blocking collectives, joined(): pieces = jax.tree.map(lambda part: lax.all_gather(part, axis), value)  20.8 us
    all_gather x1, waiting for transfers between devices, per_device(): lax.all_gather(own_student, 'mp', axis=0, tiled=True)  18.9 us
    dot_general x1, matrix products, per_device(): lax.dot_general(group_teacher, column_teacher, pair_dims, preferred_eleme...  14.8 us
    reduce_scatter x1, waiting for transfers between devices, per_device(): grad = lax.psum_scatter(result, 'mp', scatter_dimension=0, tiled=True)  13.4 us
    dot_general x1, matrix products, per_device(): lax.dot_general(own_weight, group_student, (((0,), (0,)), ((), ())), pref...  12.8 us
  transfers between devices with their start and end apart: 6, of which 6 were waited for; matrix products, arithmetic and copies ran while one was open for 5% of the time, Pallas kernels for 0%

commit v1 on v0

v1 whole, which is shorter than its diff:
```python
import functools

import jax
import jax.numpy as jnp
from jax import lax
from jax.experimental import pallas as pl
from jax.experimental.pallas import tpu as pltpu
from jax.sharding import PartitionSpec as P

MESH = pl.DeviceIdType.MESH
logit_scale = 100.0
epsilon = 1e-06
log2e = 1.4426950408889634
NEG = -1e30

PLACE = (
    (2, 3, 0), (1, 3, 0), (3, 3, 0), (0, 3, 0), (0, 0, 3), (0, 3, 1), (0, 1, 3), (0, 3, 2),
    (0, 0, 0), (0, 0, 1), (0, 1, 0), (0, 0, 2), (0, 1, 2),
)
SLOTS = 13
OWN = 8
COLS = 5
SHARE = ((0.5, 1.0, 1.0, 1.0, 0.5), (1.0, 1.0, 0.5, 1.0, 0.5))
FROM = (
    ((1, 3, 3, 8, 8, 3, 4, 11, -1, 8, 8, 9, 6), (2, 3, 3, 8, 8, 9, 4, 5, -1, 8, 8, 9, 11)),
    ((1, 3, 3, 8, 8, 9, 4, 5, -1, 8, 8, 4, 11), (2, 3, 3, 8, 8, 9, 10, 11, -1, 8, 8, 4, 6)),
)
INTO = (3, 3, 3, 8, 8, 9, 4, 11, -1, 8, 8, 8, 11)
T, S = 0, 1


def step(a, b):
    return tuple((p - q) % 4 for p, q in zip(a, b))


def partner_places():
    places = set()
    for place in PLACE:
        places |= {place, step((0, 0, 0), place)}
    for slot in range(SLOTS):
        for kind in (T, S):
            for core in (0, 1):
                if FROM[kind][core][slot] >= 0:
                    move = step(PLACE[FROM[kind][core][slot]], PLACE[slot])
                    places |= {move, step((0, 0, 0), move)}
        if INTO[slot] >= 0:
            move = step(PLACE[slot], PLACE[INTO[slot]])
            places |= {move, step((0, 0, 0), move)}
    places.discard((0, 0, 0))
    return sorted(places)


PARTNERS = partner_places()


def rows_of(slot, count=1):
    return pl.ds(slot * 256, count * 256)


def kernel(
    features, teacher, proj, out,
    s_rows, t_rows, s_score, t_score, weight, top_parts, sum_parts, col_top, col_sum,
    stat_out, stat_in, lse_out, lse_in, lse_rows, part_a, part_b, stage, joined,
    unit, norm,
    g_send, g_recv, c_send, c_recv, st_send, st_recv, l_send, l_recv,
    pa_send, pa_recv, pb_send, pb_recv, r_send, r_recv,
):
    sub, dp, mp = lax.axis_index("sub"), lax.axis_index("dp"), lax.axis_index("mp")
    x, y, z, core = sub * 2 + mp // 2, dp % 4, dp // 4, mp % 2
    other = 1 - core
    half = core * 128
    sibling = (sub, dp, (mp // 2) * 2 + other)
    rows_buf = (t_rows, s_rows)
    score_buf = (t_score, s_score)

    def device(move, to_core):
        ax, ay, az = (x + move[0]) % 4, (y + move[1]) % 4, (z + move[2]) % 4
        return (ax // 2, az * 4 + ay, (ax % 2) * 2 + to_core)

    barrier = pltpu.get_barrier_semaphore()
    for move in PARTNERS:
        for to_core in (0, 1):
            pl.semaphore_signal(barrier, inc=1, device_id=device(move, to_core), device_id_type=MESH)
    pl.semaphore_signal(barrier, inc=1, device_id=sibling, device_id_type=MESH)

    def remote(src, dst, send, recv, target):
        return pltpu.make_async_remote_copy(
            src_ref=src, dst_ref=dst, send_sem=send, recv_sem=recv, device_id=target, device_id_type=MESH
        )

    def half_rows(kind, slot, which):
        return rows_buf[kind].at[pl.ds(slot * 256 + which, 128)]

    def row_copy(kind, src_slot, slot):
        move = step(PLACE[src_slot], PLACE[slot])
        return remote(
            half_rows(kind, src_slot, half), half_rows(kind, slot, half),
            g_send.at[kind, slot], g_recv.at[kind, slot], device(move, core),
        )

    def side_copy(kind, slot, which):
        piece = half_rows(kind, slot, which)
        return remote(piece, piece, c_send.at[kind, slot], c_recv.at[kind, slot], sibling)

    def to_side(kind, slot):
        if slot < 4:
            side_copy(kind, slot, half).start()
        else:
            @pl.when(core == (1 if slot < OWN else 0))
            def _():
                side_copy(kind, slot, half).start()

    def forward(kind, slot):
        for which in (0, 1):
            children = [d for d in range(SLOTS) if FROM[kind][which][d] == slot]
            if children:
                @pl.when(core == which)
                def _(children=children):
                    for child in children:
                        row_copy(kind, slot, child).start()
        to_side(kind, slot)

    def arrive(kind, slot):
        row_copy(kind, OWN, slot).wait_recv()
        forward(kind, slot)

    def side_wait(kind, *slots):
        for slot in slots:
            if slot < 4:
                side_copy(kind, slot, 128 - half).wait_recv()
            else:
                @pl.when(core == (0 if slot < OWN else 1))
                def _(slot=slot):
                    side_copy(kind, slot, 128 - half).wait_recv()

    own_rows = pl.ds(OWN * 256 + half, 128)
    values = teacher[...].astype(jnp.float32)
    t_rows[own_rows, :] = (
        values / jnp.sqrt(jnp.sum(values * values, axis=1, keepdims=True) + epsilon)
    ).astype(jnp.bfloat16)

    pl.semaphore_wait(barrier, 2 * len(PARTNERS) + 1)
    forward(T, OWN)

    student = jnp.dot(features[...], proj[...], preferred_element_type=jnp.float32)
    length = jnp.sqrt(jnp.sum(student * student, axis=1, keepdims=True) + epsilon)
    student = student / length
    unit[...] = student
    norm[...] = jnp.broadcast_to(length, norm.shape)
    s_rows[own_rows, :] = student.astype(jnp.bfloat16)
    forward(S, OWN)

    for kind in (T, S):
        top_parts[kind] = jnp.full(top_parts.shape[1:], NEG, jnp.float32)
        sum_parts[kind] = jnp.zeros(sum_parts.shape[1:], jnp.float32)
        col_top[kind] = jnp.full(col_top.shape[1:], NEG, jnp.float32)
        col_sum[kind] = jnp.zeros(col_sum.shape[1:], jnp.float32)

    col_base = 3 + COLS * core
    pair_dims = (((1,), (1,)), ((), ()))
    lanes = lax.broadcasted_iota(jnp.int32, (256, 128), 1)

    def scores(kind, a0, na, j0, nj):
        buf, score = rows_buf[kind], score_buf[kind]

        def column(i, carry):
            j = j0 + i
            cols = buf[pl.ds(pl.multiple_of((col_base + j) * 256, 256), 256), :]
            score[pl.ds(a0 * 256, na * 256), pl.ds(pl.multiple_of(j * 256, 256), 256)] = (
                lax.dot_general(
                    buf[pl.ds(a0 * 256, na * 256), :], cols, pair_dims, preferred_element_type=jnp.float32
                ) * (logit_scale * log2e)
            )
            return carry

        lax.fori_loop(0, nj, column, 0)
        if a0 <= 3 < a0 + na and j0 == 0:
            @pl.when(core == 0)
            def _():
                tile = score[pl.ds(768, 256), pl.ds(0, 256)]
                row = lax.broadcasted_iota(jnp.int32, (256, 256), 0)
                col = lax.broadcasted_iota(jnp.int32, (256, 256), 1)
                score[pl.ds(768, 256), pl.ds(0, 256)] = jnp.where(row == col, NEG, tile)

        def totals(i, carry):
            a, j = a0 + i // nj, j0 + i % nj
            rows = pl.ds(pl.multiple_of(a * 256, 256), 256)
            cols = pl.ds(pl.multiple_of(j * 256, 256), 256)
            tile = score[rows, cols]
            top = jnp.max(tile, axis=1, keepdims=True)
            total = jnp.sum(jnp.exp2(tile - top), axis=1, keepdims=True)
            here = lanes == j
            top_parts[kind, rows, :] = jnp.where(here, top, top_parts[kind, rows, :])
            sum_parts[kind, rows, :] = jnp.where(here, total, sum_parts[kind, rows, :])
            top = jnp.max(tile, axis=0, keepdims=True)
            total = jnp.sum(jnp.exp2(tile - top), axis=0, keepdims=True)
            col_top[kind, pl.ds(a, 1), cols] = top
            col_sum[kind, pl.ds(a, 1), cols] = total
            return carry

        lax.fori_loop(0, na * nj, totals, 0)

    for kind, slot in ((T, 3), (T, 9), (T, 4), (T, 10), (S, 3), (S, 9), (S, 4), (S, 10)):
        arrive(kind, slot)
    for kind, slot in ((T, 1), (T, 2), (S, 1), (S, 2)):
        arrive(kind, slot)
    for kind in (T, S):
        side_wait(kind, 3, 4, 8, 9)
        scores(kind, 3, 1, 0, 2)
    for kind, slot in ((T, 6), (T, 11), (T, 5), (S, 6), (S, 11), (S, 5)):
        arrive(kind, slot)
    for kind in (T, S):
        side_wait(kind, 1, 2)
        scores(kind, 1, 2, 0, 2)
    for kind, slot in ((T, 0), (S, 0)):
        arrive(kind, slot)
    for kind in (T, S):
        side_wait(kind, 5, 6, 10, 11)
        scores(kind, 1, 3, 2, 2)
    for kind, slot in ((T, 7), (T, 12), (S, 7), (S, 12)):
        arrive(kind, slot)
    for kind in (T, S):
        side_wait(kind, 0)
        scores(kind, 0, 1, 0, 4)
    for kind in (T, S):
        side_wait(kind, 7, 12)
        scores(kind, 0, 4, 4, 1)

    def share(j):
        return jnp.where(core == 0, SHARE[0][j], SHARE[1][j]).astype(jnp.float32)

    share_lanes = jnp.zeros((256, 128), jnp.float32)
    for j in range(COLS):
        share_lanes = jnp.where(lanes == j, share(j), share_lanes)

    for a in range(4):
        rows = pl.ds(a * 256, 256)
        packed = jnp.zeros((256, 128), jnp.float32)
        for kind in (T, S):
            parts = top_parts[kind, rows, :]
            top = jnp.max(parts, axis=1, keepdims=True)
            total = jnp.sum(
                sum_parts[kind, rows, :] * share_lanes * jnp.exp2(parts - top), axis=1, keepdims=True
            )
            packed = jnp.where(lanes == 2 * kind, top, packed)
            packed = jnp.where(lanes == 2 * kind + 1, total, packed)
        turned = packed.T
        stat_out[a, 0] = turned[0:8, 0:128]
        stat_out[a, 1] = turned[0:8, 128:256]
    for j in range(COLS):
        cols = pl.ds(j * 256, 256)
        lines = []
        for kind in (T, S):
            parts = col_top[kind, :, cols]
            top = jnp.max(parts, axis=0, keepdims=True)
            total = jnp.sum(col_sum[kind, :, cols] * jnp.exp2(parts - top), axis=0, keepdims=True)
            lines += [top, total * share(j)]
        lines.append(jnp.zeros((4, 256), jnp.float32))
        lines = jnp.concatenate(lines, axis=0)
        stat_out[4 + j, 0] = lines[:, 0:128]
        stat_out[4 + j, 1] = lines[:, 128:256]

    def place_at(index, of_core):
        if index < 4:
            return PLACE[index]
        first, second = PLACE[index - 1], PLACE[index + 4]
        return tuple(jnp.where(of_core == 0, p, q) for p, q in zip(first, second))

    def back(move):
        return tuple(4 - m for m in move)

    def stat_copy(index, to_half):
        return remote(
            stat_out.at[index, to_half], stat_in.at[core * 9 + index],
            st_send.at[index * 2 + to_half], st_recv.at[core * 9 + index],
            device(place_at(index, core), to_half),
        )

    def unless_own(index, to_half, action, instead=None):
        if index == 4 and to_half == 1:
            pl.when(core == 0)(action)
            if instead is not None:
                pl.when(core == 1)(instead)
        else:
            action()

    def keep_stat():
        stat_in[9 + 4] = stat_out[4, 1]

    for index in range(9):
        for to_half in (0, 1):
            unless_own(index, to_half, lambda: stat_copy(index, to_half).start(), keep_stat)

    def stat_arrival(source):
        return remote(
            stat_out.at[0, 0], stat_in.at[source], st_send.at[0], st_recv.at[source], sibling
        )

    for source in range(18):
        if source == 9 + 4:
            pl.when(core == 0)(lambda: stat_arrival(13).wait_recv())
        else:
            stat_arrival(source).wait_recv()

    lines = []
    for kind in (T, S):
        tops = stat_in[:, 2 * kind, :]
        top = jnp.max(tops, axis=0, keepdims=True)
        total = jnp.sum(stat_in[:, 2 * kind + 1, :] * jnp.exp2(tops - top), axis=0, keepdims=True)
        lines.append(top + jnp.log(total) * log2e)
    lines.append(jnp.zeros((6, 128), jnp.float32))
    lse_out[...] = jnp.concatenate(lines, axis=0)

    def lse_copy(of_core, index):
        return remote(
            lse_out, lse_in.at[index, core],
            l_send.at[of_core * 9 + index], l_recv.at[index * 2 + core],
            device(back(place_at(index, jnp.int32(of_core)) if index < 4 else PLACE[index - 1 + 5 * of_core]), of_core),
        )

    def lse_arrival(index, from_half):
        return remote(
            lse_out, lse_in.at[index, from_half], l_send.at[0], l_recv.at[index * 2 + from_half], sibling
        )

    def keep_lse():
        lse_in[4, 1] = lse_out[...]

    for index in range(9):
        for of_core in (0, 1):
            if index == 4 and of_core == 1:
                pl.when(core == 0)(lambda: lse_copy(1, 4).start())
                pl.when(core == 1)(keep_lse)
            else:
                lse_copy(of_core, index).start()
    for index in range(9):
        for from_half in (0, 1):
            unless_own(index, from_half, lambda: lse_arrival(index, from_half).wait_recv())

    for a in range(4):
        lines = jnp.concatenate(
            [
                jnp.concatenate([lse_in[a, 0], lse_in[a, 1]], axis=1),
                jnp.zeros((120, 256), jnp.float32),
            ],
            axis=0,
        ).T
        for kind in (T, S):
            lse_rows[kind, pl.ds(a * 256, 256), :] = jnp.broadcast_to(lines[:, kind:kind + 1], (256, 128))

    def weights(a):
        for j in range(COLS):
            for side in (0, 1):
                def chunk(i, carry):
                    rows = pl.ds(pl.multiple_of(a * 256 + i * 64, 64), 64)
                    cols = pl.ds(j * 256 + side * 128, 128)
                    s_tile, t_tile = s_score[rows, cols], t_score[rows, cols]
                    value = (
                        jnp.exp2(s_tile - lse_rows[S, rows, :])
                        + jnp.exp2(s_tile - lse_in[4 + j, side, S:S + 1, :])
                        - jnp.exp2(t_tile - lse_rows[T, rows, :])
                        - jnp.exp2(t_tile - lse_in[4 + j, side, T:T + 1, :])
                    )
                    weight[rows, cols] = (value * share(j)).astype(jnp.bfloat16)
                    return carry

                lax.fori_loop(0, 4, chunk, 0)

    def part_a_copy(a):
        piece = part_a.at[core, a, other]
        return remote(piece, piece, pa_send.at[a], pa_recv.at[a], sibling)

    def part_b_copy(j):
        piece = part_b.at[core, j, other]
        return remote(piece, piece, pb_send.at[j], pb_recv.at[j], sibling)

    def part_a_arrival(a):
        piece = part_a.at[other, a, core]
        return remote(piece, piece, pa_send.at[a], pa_recv.at[a], sibling)

    def part_b_arrival(j):
        piece = part_b.at[other, j, core]
        return remote(piece, piece, pb_send.at[j], pb_recv.at[j], sibling)

    for a in range(4):
        weights(a)
        term = jnp.dot(
            weight[pl.ds(a * 256, 256), :],
            s_rows[pl.ds(pl.multiple_of(col_base * 256, 256), COLS * 256), :],
            preferred_element_type=jnp.float32,
        ).astype(jnp.bfloat16)
        part_a[core, a] = term.reshape(2, 128, 1024)
        part_a_copy(a).start()

    def slot_base(slot):
        terms = []
        if slot < 4:
            terms += [part_a.at[0, slot, core], part_a.at[1, slot, core]]
        if slot >= 3:
            terms.append(part_b.at[(slot - 3) // 5, (slot - 3) % 5, core])
        return terms

    def slot_wait(slot):
        if slot < 4:
            part_a_arrival(slot).wait_recv()
        if slot >= 3:
            @pl.when(core != (slot - 3) // 5)
            def _():
                part_b_arrival((slot - 3) % 5).wait_recv()

    def sum_copy(slot, src):
        return remote(
            src, stage.at[slot], r_send.at[slot], r_recv.at[slot],
            device(step(PLACE[slot], PLACE[INTO[slot]]), core),
        )

    def slot_terms(slot):
        slot_wait(slot)
        terms = slot_base(slot)
        for child in range(SLOTS):
            if INTO[child] == slot:
                sum_copy(child, stage.at[child]).wait_recv()
                terms.append(stage.at[child])
        return terms

    def send_sum(slot):
        terms = slot_terms(slot)
        if len(terms) == 1:
            sum_copy(slot, terms[0]).start()
        else:
            joined[slot] = functools.reduce(
                lambda p, q: p + q, [term[...].astype(jnp.float32) for term in terms]
            ).astype(jnp.bfloat16)
            sum_copy(slot, joined.at[slot]).start()

    def columns(j):
        term = lax.dot_general(
            weight[:, pl.ds(j * 256, 256)], s_rows[pl.ds(0, 1024), :],
            (((0,), (0,)), ((), ())), preferred_element_type=jnp.float32,
        ).astype(jnp.bfloat16)
        part_b[core, j] = term.reshape(2, 128, 1024)
        part_b_copy(j).start()

    send_sum(0)
    columns(4)
    send_sum(1)
    send_sum(2)
    columns(3)
    send_sum(7)
    send_sum(12)
    columns(2)
    send_sum(6)
    columns(1)
    send_sum(5)
    columns(0)
    send_sum(10)
    for slot in (4, 9, 11, 3):
        send_sum(slot)

    terms = slot_terms(OWN)
    grad = logit_scale * functools.reduce(
        lambda p, q: p + q, [term[...].astype(jnp.float32) for term in terms]
    )
    student = unit[...]
    along = jnp.sum(student * grad, axis=1, keepdims=True)
    d_student = ((grad - student * along) / norm[:, 0:1]).astype(jnp.bfloat16)
    out[...] = lax.dot_general(d_student, proj[...], pair_dims, preferred_element_type=jnp.float32)

    for kind in (T, S):
        for slot in range(SLOTS):
            if slot != OWN:
                row_copy(kind, OWN, slot).wait_send()
            if slot < 4:
                side_copy(kind, slot, half).wait_send()
            else:
                @pl.when(core == (1 if slot < OWN else 0))
                def _(kind=kind, slot=slot):
                    side_copy(kind, slot, half).wait_send()
    for index in range(9):
        for to_half in (0, 1):
            unless_own(index, to_half, lambda: stat_copy(index, to_half).wait_send())
        for of_core in (0, 1):
            if index == 4 and of_core == 1:
                pl.when(core == 0)(lambda: lse_copy(1, 4).wait_send())
            else:
                lse_copy(of_core, index).wait_send()
    for a in range(4):
        part_a_copy(a).wait_send()
    for j in range(COLS):
        part_b_copy(j).wait_send()
    for slot in range(SLOTS):
        if slot != OWN:
            sum_copy(slot, joined.at[slot]).wait_send()


def per_device(features, teacher, proj):
    bf16, f32 = jnp.bfloat16, jnp.float32
    vmem = pl.BlockSpec(memory_space=pltpu.VMEM)
    dma = pltpu.SemaphoreType.DMA
    return pl.pallas_call(
        kernel,
        out_shape=jax.ShapeDtypeStruct((128, 1024), f32),
        in_specs=[vmem] * 3,
        out_specs=vmem,
        scratch_shapes=[
            pltpu.VMEM((SLOTS * 256, 1024), bf16),
            pltpu.VMEM((SLOTS * 256, 1024), bf16),
            pltpu.VMEM((1024, COLS * 256), f32),
            pltpu.VMEM((1024, COLS * 256), f32),
            pltpu.VMEM((1024, COLS * 256), bf16),
            pltpu.VMEM((2, 1024, 128), f32),
            pltpu.VMEM((2, 1024, 128), f32),
            pltpu.VMEM((2, 8, COLS * 256), f32),
            pltpu.VMEM((2, 8, COLS * 256), f32),
            pltpu.VMEM((9, 2, 8, 128), f32),
            pltpu.VMEM((18, 8, 128), f32),
            pltpu.VMEM((8, 128), f32),
            pltpu.VMEM((9, 2, 8, 128), f32),
            pltpu.VMEM((2, 1024, 128), f32),
            pltpu.VMEM((2, 4, 2, 128, 1024), bf16),
            pltpu.VMEM((2, COLS, 2, 128, 1024), bf16),
            pltpu.VMEM((SLOTS, 128, 1024), bf16),
            pltpu.VMEM((SLOTS, 128, 1024), bf16),
            pltpu.VMEM((128, 1024), f32),
            pltpu.VMEM((128, 128), f32),
            dma((2, SLOTS)), dma((2, SLOTS)), dma((2, SLOTS)), dma((2, SLOTS)),
            dma((18,)), dma((18,)), dma((18,)), dma((18,)),
            dma((4,)), dma((4,)), dma((COLS,)), dma((COLS,)), dma((SLOTS,)), dma((SLOTS,)),
        ],
        compiler_params=pltpu.CompilerParams(
            collective_id=0, has_side_effects=True, vmem_limit_bytes=60 * 2**20
        ),
        cost_estimate=pl.CostEstimate(flops=9_000_000_000, bytes_accessed=4_000_000, transcendentals=9_000_000),
    )(features, teacher, proj)


def solution(mesh):
    in_specs = (P(("sub", "dp", "mp"), None), P(("sub", "dp", "mp"), None), P())
    out_specs = P(("sub", "dp", "mp"), None)
    return jax.shard_map(
        per_device, mesh=mesh, in_specs=in_specs, out_specs=out_specs, check_vma=False
    )
```

time: 596 us -> 105 us (0.18)
  waiting for transfers between devices: 486 us -> 0 us
  Pallas kernels: 0 us -> 103 us
  matrix products: 51.7 us -> 0 us
  blocking collectives: 20.8 us -> 0 us
  other arithmetic: 19.9 us -> 0 us
  between operations: 13.6 us -> 0.01 us
    all_gather x4 -> x0, waiting for transfers between devices: 243 us -> none  [the longest x1 108 us: per_device(): lax.all_gather(own_student, ('sub', 'dp'), axis=0, tiled=True)]
    reduce_scatter x2 -> x0, waiting for transfers between devices: 241 us -> none  [the longest x1 228 us: per_device(): lax.psum_scatter(lax.dot_general(own_weight, group_student, (((0,), (0,))...]
    pallas_call x0 -> x1, Pallas kernels: none -> 103 us  [per_device(): pl.pallas_call(kernel, out_shape=jax.ShapeDtypeStruct((128, 1024), f32),...]
    dot_general x6 -> x0, matrix products: 51.7 us -> none  [the longest x1 14.8 us: per_device(): lax.dot_general(group_teacher, column_teacher, pair_dims, preferred_eleme...]
    all_gather x4 -> x0, blocking collectives: 20.8 us -> none  [joined(): pieces = jax.tree.map(lambda part: lax.all_gather(part, axis), value)]
    convert_element_type x3 -> x0, other arithmetic: 11 us -> none  [the longest x1 8.4 us: per_device(): own_weight = jnp.where(diagonal_mask, 0.0, values).astype(jnp.bfloat16)]
    reduce_sum x3 -> x0, other arithmetic: 8.8 us -> none  [the longest x1 6.3 us: partial_totals(): jnp.sum(jnp.where(diagonal_mask, 0.0, jnp.exp(score - row_top[:, None])),...]
  transfers between devices with their start and end apart: 6 -> 0, of which waited for: 6 -> 0; matrix products, arithmetic and copies ran while one was open for 5% -> 0% of each run, Pallas kernels for 0% -> 0%
where the time goes in v1:
time: 105 us
  Pallas kernels  103 us (98%)
  local copies, waits for them, and re-layouts  1.89 us (2%)
    pallas_call x1, Pallas kernels, per_device(): pl.pallas_call(kernel, out_shape=jax.ShapeDtypeStruct((128, 1024), f32),...  103 us

profile of v1, /device:TPU:0, one launch (start us, length us, event | category | flops | bytes accessed | tf_op | source)
XLA Modules:
  0.0 105.1 jit_solution(16078107905144892645)
XLA Ops:
  0.0 103.2 %shard_map.37 = f32[128,1024]{1,0:T(8,128)} custom-call(bf16[128,1024]{1,0:T(8,128)(2,1)} %features.1, bf16[128,1024]{1,0:T(8,128)(2,1)} %teacher.1, bf16[1024,1024]{1,0:T(8,128)(2,1)} %proj.1), custom_call_target="tpu_custom_call" | custom-call | flops 8999999488 | bytes 4000000 | tf_op jit(solution)/shard_map/pallas_call | solution.py:500
  103.2 1.9 %copy.5 = f32[128,1024]{1,0:T(8,128)} copy(f32[128,1024]{1,0:T(8,128)} %shard_map.37) | data formatting | bytes 1048576

commit v2 on v1

--- a/solution.py
+++ b/solution.py
@@ -25,7 +25,10 @@
     ((1, 3, 3, 8, 8, 3, 4, 11, -1, 8, 8, 9, 6), (2, 3, 3, 8, 8, 9, 4, 5, -1, 8, 8, 9, 11)),
     ((1, 3, 3, 8, 8, 9, 4, 5, -1, 8, 8, 4, 11), (2, 3, 3, 8, 8, 9, 10, 11, -1, 8, 8, 4, 6)),
 )
-INTO = (3, 3, 3, 8, 8, 9, 4, 11, -1, 8, 8, 8, 11)
+INTO = (
+    ((1, 3, 3, 8, 8, 9, 10, 11, -1, 8, 8, 8, 11), (2, 3, 3, 8, 8, 9, 10, 11, -1, 8, 8, 8, 11)),
+    ((1, 3, 3, 8, 8, 3, 4, 11, -1, 8, 8, 8, 11), (2, 3, 3, 8, 8, 3, 4, 11, -1, 8, 8, 8, 11)),
+)
 T, S = 0, 1
 
 
@@ -33,24 +36,7 @@
     return tuple((p - q) % 4 for p, q in zip(a, b))
 
 
-def partner_places():
-    places = set()
-    for place in PLACE:
-        places |= {place, step((0, 0, 0), place)}
-    for slot in range(SLOTS):
-        for kind in (T, S):
-            for core in (0, 1):
-                if FROM[kind][core][slot] >= 0:
-                    move = step(PLACE[FROM[kind][core][slot]], PLACE[slot])
-                    places |= {move, step((0, 0, 0), move)}
-        if INTO[slot] >= 0:
-            move = step(PLACE[slot], PLACE[INTO[slot]])
-            places |= {move, step((0, 0, 0), move)}
-    places.discard((0, 0, 0))
-    return sorted(places)
-
-
-PARTNERS = partner_places()
+NEIGHBOURS = ((1, 0, 0), (3, 0, 0), (0, 1, 0), (0, 3, 0), (0, 0, 1), (0, 0, 3))
 
 
 def rows_of(slot, count=1):
@@ -78,9 +64,8 @@
         return (ax // 2, az * 4 + ay, (ax % 2) * 2 + to_core)
 
     barrier = pltpu.get_barrier_semaphore()
-    for move in PARTNERS:
-        for to_core in (0, 1):
-            pl.semaphore_signal(barrier, inc=1, device_id=device(move, to_core), device_id_type=MESH)
+    for move in NEIGHBOURS:
+        pl.semaphore_signal(barrier, inc=1, device_id=device(move, core), device_id_type=MESH)
     pl.semaphore_signal(barrier, inc=1, device_id=sibling, device_id_type=MESH)
 
     def remote(src, dst, send, recv, target):
@@ -139,7 +124,7 @@
         values / jnp.sqrt(jnp.sum(values * values, axis=1, keepdims=True) + epsilon)
     ).astype(jnp.bfloat16)
 
-    pl.semaphore_wait(barrier, 2 * len(PARTNERS) + 1)
+    pl.semaphore_wait(barrier, len(NEIGHBOURS) + 1)
     forward(T, OWN)
 
     student = jnp.dot(features[...], proj[...], preferred_element_type=jnp.float32)
@@ -229,6 +214,7 @@
     def share(j):
         return jnp.where(core == 0, SHARE[0][j], SHARE[1][j]).astype(jnp.float32)
 
+    shares = [share(j) for j in range(COLS)]
     share_lanes = jnp.zeros((256, 128), jnp.float32)
     for j in range(COLS):
         share_lanes = jnp.where(lanes == j, share(j), share_lanes)
@@ -351,8 +337,8 @@
     def weights(a):
         for j in range(COLS):
             for side in (0, 1):
-                def chunk(i, carry):
-                    rows = pl.ds(pl.multiple_of(a * 256 + i * 64, 64), 64)
+                for i in range(4):
+                    rows = pl.ds(a * 256 + i * 64, 64)
                     cols = pl.ds(j * 256 + side * 128, 128)
                     s_tile, t_tile = s_score[rows, cols], t_score[rows, cols]
                     value = (
@@ -361,10 +347,7 @@
                         - jnp.exp2(t_tile - lse_rows[T, rows, :])
                         - jnp.exp2(t_tile - lse_in[4 + j, side, T:T + 1, :])
                     )
-                    weight[rows, cols] = (value * share(j)).astype(jnp.bfloat16)
-                    return carry
-
-                lax.fori_loop(0, 4, chunk, 0)
+                    weight[rows, cols] = (value * shares[j]).astype(jnp.bfloat16)
 
     def part_a_copy(a):
         piece = part_a.at[core, a, other]
@@ -382,25 +365,26 @@
         piece = part_b.at[other, j, core]
         return remote(piece, piece, pb_send.at[j], pb_recv.at[j], sibling)
 
-    for a in range(4):
-        weights(a)
+    def rows_term(a):
         term = jnp.dot(
             weight[pl.ds(a * 256, 256), :],
             s_rows[pl.ds(pl.multiple_of(col_base * 256, 256), COLS * 256), :],
             preferred_element_type=jnp.float32,
         ).astype(jnp.bfloat16)
         part_a[core, a] = term.reshape(2, 128, 1024)
-        part_a_copy(a).start()
-
-    def slot_base(slot):
-        terms = []
-        if slot < 4:
-            terms += [part_a.at[0, slot, core], part_a.at[1, slot, core]]
-        if slot >= 3:
-            terms.append(part_b.at[(slot - 3) // 5, (slot - 3) % 5, core])
-        return terms
-
-    def slot_wait(slot):
+
+    def columns_term(j):
+        term = lax.dot_general(
+            weight[:, pl.ds(j * 256, 256)], s_rows[pl.ds(0, 1024), :],
+            (((0,), (0,)), ((), ())), preferred_element_type=jnp.float32,
+        ).astype(jnp.bfloat16)
+        part_b[core, j] = term.reshape(2, 128, 1024)
+        part_b_copy(j).start()
+
+    def piece_of(ref, piece):
+        return ref.at[pl.ds(piece * 64, 64), :]
+
+    def slot_ready(slot):
         if slot < 4:
             part_a_arrival(slot).wait_recv()
         if slot >= 3:
@@ -408,58 +392,89 @@
             def _():
                 part_b_arrival((slot - 3) % 5).wait_recv()
 
-    def sum_copy(slot, src):
+    def sum_copy(which, slot, piece, src):
+        into = INTO[which][piece][slot]
         return remote(
-            src, stage.at[slot], r_send.at[slot], r_recv.at[slot],
-            device(step(PLACE[slot], PLACE[INTO[slot]]), core),
-        )
-
-    def slot_terms(slot):
-        slot_wait(slot)
-        terms = slot_base(slot)
+            piece_of(src, piece), piece_of(stage.at[slot], piece),
+            r_send.at[slot * 2 + piece], r_recv.at[slot * 2 + piece],
+            device(step(PLACE[slot], PLACE[into]), core),
+        )
+
+    def slot_terms(which, slot, piece):
+        terms = []
+        if slot < 4:
+            terms += [part_a.at[0, slot, core], part_a.at[1, slot, core]]
+        if slot >= 3:
+            terms.append(part_b.at[(slot - 3) // 5, (slot - 3) % 5, core])
         for child in range(SLOTS):
-            if INTO[child] == slot:
-                sum_copy(child, stage.at[child]).wait_recv()
+            if INTO[which][piece][child] == slot:
+                sum_copy(which, child, piece, stage.at[child]).wait_recv()
                 terms.append(stage.at[child])
         return terms
 
-    def send_sum(slot):
-        terms = slot_terms(slot)
-        if len(terms) == 1:
-            sum_copy(slot, terms[0]).start()
+    def added(terms, piece):
+        return functools.reduce(
+            lambda p, q: p + q, [piece_of(term, piece)[...].astype(jnp.float32) for term in terms]
+        )
+
+    def send_sum(slot, *pieces):
+        def send(which):
+            for piece in pieces:
+                terms = slot_terms(which, slot, piece)
+                if len(terms) == 1:
+                    sum_copy(which, slot, piece, terms[0]).start()
+                else:
+                    piece_of(joined.at[slot], piece)[...] = added(terms, piece).astype(jnp.bfloat16)
+                    sum_copy(which, slot, piece, joined.at[slot]).start()
+
+        routes = [
+            [(INTO[which][piece][slot], [c for c in range(SLOTS) if INTO[which][piece][c] == slot]) for piece in pieces]
+            for which in (0, 1)
+        ]
+        if routes[0] == routes[1]:
+            send(0)
         else:
-            joined[slot] = functools.reduce(
-                lambda p, q: p + q, [term[...].astype(jnp.float32) for term in terms]
-            ).astype(jnp.bfloat16)
-            sum_copy(slot, joined.at[slot]).start()
-
-    def columns(j):
-        term = lax.dot_general(
-            weight[:, pl.ds(j * 256, 256)], s_rows[pl.ds(0, 1024), :],
-            (((0,), (0,)), ((), ())), preferred_element_type=jnp.float32,
-        ).astype(jnp.bfloat16)
-        part_b[core, j] = term.reshape(2, 128, 1024)
-        part_b_copy(j).start()
-
-    send_sum(0)
-    columns(4)
-    send_sum(1)
-    send_sum(2)
-    columns(3)
-    send_sum(7)
-    send_sum(12)
-    columns(2)
-    send_sum(6)
-    columns(1)
-    send_sum(5)
-    columns(0)
-    send_sum(10)
-    for slot in (4, 9, 11, 3):
-        send_sum(slot)
-
-    terms = slot_terms(OWN)
-    grad = logit_scale * functools.reduce(
-        lambda p, q: p + q, [term[...].astype(jnp.float32) for term in terms]
+            pl.when(core == 0)(lambda: send(0))
+            pl.when(core == 1)(lambda: send(1))
+
+    weights(0)
+    for a in range(4):
+        rows_term(a)
+        if a < 3:
+            weights(a + 1)
+        part_a_copy(a).start()
+        if a == 2:
+            slot_ready(0)
+            send_sum(0, 0, 1)
+            slot_ready(1)
+            send_sum(1, 1)
+        if a == 3:
+            slot_ready(2)
+            send_sum(2, 0)
+    columns_term(4)
+    columns_term(3)
+    for slot in (7, 12):
+        slot_ready(slot)
+        send_sum(slot, 0, 1)
+    send_sum(1, 0)
+    send_sum(2, 1)
+    columns_term(2)
+    for slot in (6, 11):
+        slot_ready(slot)
+    send_sum(6, 0, 1)
+    columns_term(1)
+    for slot in (5, 10):
+        slot_ready(slot)
+    send_sum(5, 0, 1)
+    columns_term(0)
+    for slot in (4, 9, 3, 8):
+        slot_ready(slot)
+    for piece in (0, 1):
+        for slot in (11, 10, 4, 9, 3):
+            send_sum(slot, piece)
+
+    grad = logit_scale * jnp.concatenate(
+        [added(slot_terms(0, OWN, piece), piece) for piece in (0, 1)], axis=0
     )
     student = unit[...]
     along = jnp.sum(student * grad, axis=1, keepdims=True)
@@ -490,7 +505,8 @@
         part_b_copy(j).wait_send()
     for slot in range(SLOTS):
         if slot != OWN:
-            sum_copy(slot, joined.at[slot]).wait_send()
+            for piece in (0, 1):
+                sum_copy(0, slot, piece, joined.at[slot]).wait_send()
 
 
 def per_device(features, teacher, proj):
@@ -525,7 +541,7 @@
             pltpu.VMEM((128, 128), f32),
             dma((2, SLOTS)), dma((2, SLOTS)), dma((2, SLOTS)), dma((2, SLOTS)),
             dma((18,)), dma((18,)), dma((18,)), dma((18,)),
-            dma((4,)), dma((4,)), dma((COLS,)), dma((COLS,)), dma((SLOTS,)), dma((SLOTS,)),
+            dma((4,)), dma((4,)), dma((COLS,)), dma((COLS,)), dma((2 * SLOTS,)), dma((2 * SLOTS,)),
         ],
         compiler_params=pltpu.CompilerParams(
             collective_id=0, has_side_effects=True, vmem_limit_bytes=60 * 2**20

time: 105 us -> 98.3 us (0.936); the launches traced: 105 us -> 97.1 us
  Pallas kernels: 103 us -> 95.2 us
    pallas_call x1, Pallas kernels: 103 us -> 95.2 us  [per_device(): pl.pallas_call(kernel, out_shape=jax.ShapeDtypeStruct((128, 1024), f32),...]
where the time goes in v2:
time: 98.3 us; the launch traced here: 97.1 us
  Pallas kernels  95.2 us (97%)
  local copies, waits for them, and re-layouts  1.89 us (2%)
    pallas_call x1, Pallas kernels, per_device(): pl.pallas_call(kernel, out_shape=jax.ShapeDtypeStruct((128, 1024), f32),...  95.2 us

profile of v2, /device:TPU:0, one launch (start us, length us, event | category | flops | bytes accessed | tf_op | source)
XLA Modules:
  0.0 97.1 jit_solution(4115696934444371846)
XLA Ops:
  0.0 95.2 %shard_map.37 = f32[128,1024]{1,0:T(8,128)} custom-call(bf16[128,1024]{1,0:T(8,128)(2,1)} %features.1, bf16[128,1024]{1,0:T(8,128)(2,1)} %teacher.1, bf16[1024,1024]{1,0:T(8,128)(2,1)} %proj.1), custom_call_target="tpu_custom_call" | custom-call | flops 8999999488 | bytes 4000000 | tf_op jit(solution)/shard_map/pallas_call | solution.py:516
  95.2 1.9 %copy.5 = f32[128,1024]{1,0:T(8,128)} copy(f32[128,1024]{1,0:T(8,128)} %shard_map.37) | data formatting | bytes 1048576

commit v3 on v2

--- a/solution.py
+++ b/solution.py
@@ -22,12 +22,21 @@
 COLS = 5
 SHARE = ((0.5, 1.0, 1.0, 1.0, 0.5), (1.0, 1.0, 0.5, 1.0, 0.5))
 FROM = (
-    ((1, 3, 3, 8, 8, 3, 4, 11, -1, 8, 8, 9, 6), (2, 3, 3, 8, 8, 9, 4, 5, -1, 8, 8, 9, 11)),
-    ((1, 3, 3, 8, 8, 9, 4, 5, -1, 8, 8, 4, 11), (2, 3, 3, 8, 8, 9, 10, 11, -1, 8, 8, 4, 6)),
+    ((2, 3, 3, 8, 8, 9, 4, 5, -1, 8, 8, 4, 6), (2, 3, 3, 8, 8, 9, 10, 11, -1, 8, 8, 9, 6)),
+    ((2, 3, 3, 8, 8, 9, 10, 11, -1, 8, 8, 9, 11), (2, 3, 3, 8, 8, 3, 4, 5, -1, 8, 8, 9, 11)),
+    ((1, 3, 3, 8, 8, 3, 4, 11, -1, 8, 8, 4, 11), (1, 3, 3, 8, 8, 9, 4, 11, -1, 8, 8, 4, 11)),
+    ((1, 3, 3, 8, 8, 9, 4, 5, -1, 8, 8, 9, 6), (1, 3, 3, 8, 8, 9, 4, 5, -1, 8, 8, 4, 6)),
+)
+FIRST = (
+    "S3", "V10", "V4", "V9", "S4", "T3", "T4", "T9", "U4", "V3", "S9", "T10", "U3", "S10", "U10", "U9",
 )
 INTO = (
-    ((1, 3, 3, 8, 8, 9, 10, 11, -1, 8, 8, 8, 11), (2, 3, 3, 8, 8, 9, 10, 11, -1, 8, 8, 8, 11)),
-    ((1, 3, 3, 8, 8, 3, 4, 11, -1, 8, 8, 8, 11), (2, 3, 3, 8, 8, 3, 4, 11, -1, 8, 8, 8, 11)),
+    ((2, 3, 3, 8, 8, 9, 4, 5, -1, 8, 8, 9, 10), (2, 3, 3, 8, 8, 9, 4, 11, -1, 8, 8, 4, 11)),
+    ((1, 3, 3, 8, 8, 9, 4, 5, -1, 8, 8, 9, 10), (1, 3, 3, 8, 8, 9, 4, 11, -1, 8, 8, 4, 6)),
+)
+ORDER = (
+    "W0", "A0", "W1", "W2", "W3", "B4", "0.0", "A1", "7.0", "7.1", "0.1", "12.1", "A2", "B2", "12.0", "B3",
+    "5.1", "6.0", "1.0", "2.0", "B1", "A3", "5.0", "1.1", "11.0", "11.1", "6.1", "B0", "2.1", "10.1", "4.0", "9.1", "3.0", "10.0", "9.0", "3.1", "4.1",
 )
 T, S = 0, 1
 
@@ -44,13 +53,21 @@
 
 
 def kernel(
-    features, teacher, proj, out,
+    features_in, teacher_in, proj_in, out,
+    features, teacher, proj,
     s_rows, t_rows, s_score, t_score, weight, top_parts, sum_parts, col_top, col_sum,
     stat_out, stat_in, lse_out, lse_in, lse_rows, part_a, part_b, stage, joined,
     unit, norm,
     g_send, g_recv, c_send, c_recv, st_send, st_recv, l_send, l_recv,
-    pa_send, pa_recv, pb_send, pb_recv, r_send, r_recv,
+    pa_send, pa_recv, pb_send, pb_recv, r_send, r_recv, in_sem,
 ):
+    loads = [
+        pltpu.make_async_copy(src, dst, in_sem.at[i])
+        for i, (src, dst) in enumerate(((teacher_in, teacher), (features_in, features), (proj_in, proj)))
+    ]
+    for load in loads:
+        load.start()
+
     sub, dp, mp = lax.axis_index("sub"), lax.axis_index("dp"), lax.axis_index("mp")
     x, y, z, core = sub * 2 + mp // 2, dp % 4, dp // 4, mp % 2
     other = 1 - core
@@ -73,67 +90,73 @@
             src_ref=src, dst_ref=dst, send_sem=send, recv_sem=recv, device_id=target, device_id_type=MESH
         )
 
-    def half_rows(kind, slot, which):
-        return rows_buf[kind].at[pl.ds(slot * 256 + which, 128)]
-
-    def row_copy(kind, src_slot, slot):
+    def piece_rows(q, slot, which):
+        return rows_buf[q // 2].at[pl.ds(slot * 256 + which + (q % 2) * 64, 64)]
+
+    def row_copy(q, src_slot, slot):
         move = step(PLACE[src_slot], PLACE[slot])
         return remote(
-            half_rows(kind, src_slot, half), half_rows(kind, slot, half),
-            g_send.at[kind, slot], g_recv.at[kind, slot], device(move, core),
-        )
-
-    def side_copy(kind, slot, which):
-        piece = half_rows(kind, slot, which)
-        return remote(piece, piece, c_send.at[kind, slot], c_recv.at[kind, slot], sibling)
-
-    def to_side(kind, slot):
+            piece_rows(q, src_slot, half), piece_rows(q, slot, half),
+            g_send.at[q, slot], g_recv.at[q, slot], device(move, core),
+        )
+
+    def side_copy(q, slot, which):
+        piece = piece_rows(q, slot, which)
+        return remote(piece, piece, c_send.at[q, slot], c_recv.at[q, slot], sibling)
+
+    def to_side(q, slot):
         if slot < 4:
-            side_copy(kind, slot, half).start()
+            side_copy(q, slot, half).start()
         else:
             @pl.when(core == (1 if slot < OWN else 0))
             def _():
-                side_copy(kind, slot, half).start()
-
-    def forward(kind, slot):
-        for which in (0, 1):
-            children = [d for d in range(SLOTS) if FROM[kind][which][d] == slot]
-            if children:
-                @pl.when(core == which)
-                def _(children=children):
-                    for child in children:
-                        row_copy(kind, slot, child).start()
-        to_side(kind, slot)
-
-    def arrive(kind, slot):
-        row_copy(kind, OWN, slot).wait_recv()
-        forward(kind, slot)
+                side_copy(q, slot, half).start()
+
+    def start_rows(q, slot, children):
+        for child in children:
+            row_copy(q, slot, child).start()
+
+    def arrive(q, slot):
+        row_copy(q, OWN, slot).wait_recv()
+        children = [[d for d in range(SLOTS) if FROM[q][which][d] == slot] for which in (0, 1)]
+        if children[0] == children[1]:
+            start_rows(q, slot, children[0])
+        else:
+            for which in (0, 1):
+                if children[which]:
+                    pl.when(core == which)(lambda: start_rows(q, slot, children[which]))
+        to_side(q, slot)
 
     def side_wait(kind, *slots):
         for slot in slots:
-            if slot < 4:
-                side_copy(kind, slot, 128 - half).wait_recv()
-            else:
-                @pl.when(core == (0 if slot < OWN else 1))
-                def _(slot=slot):
-                    side_copy(kind, slot, 128 - half).wait_recv()
+            for q in (2 * kind, 2 * kind + 1):
+                if slot < 4:
+                    side_copy(q, slot, 128 - half).wait_recv()
+                else:
+                    @pl.when(core == (0 if slot < OWN else 1))
+                    def _(slot=slot, q=q):
+                        side_copy(q, slot, 128 - half).wait_recv()
 
     own_rows = pl.ds(OWN * 256 + half, 128)
+    loads[0].wait()
     values = teacher[...].astype(jnp.float32)
     t_rows[own_rows, :] = (
         values / jnp.sqrt(jnp.sum(values * values, axis=1, keepdims=True) + epsilon)
     ).astype(jnp.bfloat16)
-
-    pl.semaphore_wait(barrier, len(NEIGHBOURS) + 1)
-    forward(T, OWN)
-
+    loads[1].wait()
+    loads[2].wait()
     student = jnp.dot(features[...], proj[...], preferred_element_type=jnp.float32)
     length = jnp.sqrt(jnp.sum(student * student, axis=1, keepdims=True) + epsilon)
     student = student / length
     unit[...] = student
     norm[...] = jnp.broadcast_to(length, norm.shape)
     s_rows[own_rows, :] = student.astype(jnp.bfloat16)
-    forward(S, OWN)
+
+    pl.semaphore_wait(barrier, len(NEIGHBOURS) + 1)
+    for name in FIRST:
+        start_rows("TUSV".index(name[0]), OWN, (int(name[1:]),))
+    for q in range(4):
+        to_side(q, OWN)
 
     for kind in (T, S):
         top_parts[kind] = jnp.full(top_parts.shape[1:], NEG, jnp.float32)
@@ -145,79 +168,75 @@
     pair_dims = (((1,), (1,)), ((), ()))
     lanes = lax.broadcasted_iota(jnp.int32, (256, 128), 1)
 
-    def scores(kind, a0, na, j0, nj):
-        buf, score = rows_buf[kind], score_buf[kind]
-
-        def column(i, carry):
-            j = j0 + i
-            cols = buf[pl.ds(pl.multiple_of((col_base + j) * 256, 256), 256), :]
-            score[pl.ds(a0 * 256, na * 256), pl.ds(pl.multiple_of(j * 256, 256), 256)] = (
-                lax.dot_general(
-                    buf[pl.ds(a0 * 256, na * 256), :], cols, pair_dims, preferred_element_type=jnp.float32
-                ) * (logit_scale * log2e)
-            )
-            return carry
-
-        lax.fori_loop(0, nj, column, 0)
-        if a0 <= 3 < a0 + na and j0 == 0:
-            @pl.when(core == 0)
-            def _():
-                tile = score[pl.ds(768, 256), pl.ds(0, 256)]
-                row = lax.broadcasted_iota(jnp.int32, (256, 256), 0)
-                col = lax.broadcasted_iota(jnp.int32, (256, 256), 1)
-                score[pl.ds(768, 256), pl.ds(0, 256)] = jnp.where(row == col, NEG, tile)
-
-        def totals(i, carry):
-            a, j = a0 + i // nj, j0 + i % nj
-            rows = pl.ds(pl.multiple_of(a * 256, 256), 256)
-            cols = pl.ds(pl.multiple_of(j * 256, 256), 256)
-            tile = score[rows, cols]
-            top = jnp.max(tile, axis=1, keepdims=True)
-            total = jnp.sum(jnp.exp2(tile - top), axis=1, keepdims=True)
-            here = lanes == j
-            top_parts[kind, rows, :] = jnp.where(here, top, top_parts[kind, rows, :])
-            sum_parts[kind, rows, :] = jnp.where(here, total, sum_parts[kind, rows, :])
-            top = jnp.max(tile, axis=0, keepdims=True)
-            total = jnp.sum(jnp.exp2(tile - top), axis=0, keepdims=True)
-            col_top[kind, pl.ds(a, 1), cols] = top
-            col_sum[kind, pl.ds(a, 1), cols] = total
-            return carry
-
-        lax.fori_loop(0, na * nj, totals, 0)
-
-    for kind, slot in ((T, 3), (T, 9), (T, 4), (T, 10), (S, 3), (S, 9), (S, 4), (S, 10)):
-        arrive(kind, slot)
-    for kind, slot in ((T, 1), (T, 2), (S, 1), (S, 2)):
-        arrive(kind, slot)
-    for kind in (T, S):
-        side_wait(kind, 3, 4, 8, 9)
-        scores(kind, 3, 1, 0, 2)
-    for kind, slot in ((T, 6), (T, 11), (T, 5), (S, 6), (S, 11), (S, 5)):
-        arrive(kind, slot)
-    for kind in (T, S):
-        side_wait(kind, 1, 2)
-        scores(kind, 1, 2, 0, 2)
-    for kind, slot in ((T, 0), (S, 0)):
-        arrive(kind, slot)
-    for kind in (T, S):
-        side_wait(kind, 5, 6, 10, 11)
-        scores(kind, 1, 3, 2, 2)
-    for kind, slot in ((T, 7), (T, 12), (S, 7), (S, 12)):
-        arrive(kind, slot)
-    for kind in (T, S):
-        side_wait(kind, 0)
-        scores(kind, 0, 1, 0, 4)
-    for kind in (T, S):
-        side_wait(kind, 7, 12)
-        scores(kind, 0, 4, 4, 1)
-
     def share(j):
         return jnp.where(core == 0, SHARE[0][j], SHARE[1][j]).astype(jnp.float32)
 
     shares = [share(j) for j in range(COLS)]
-    share_lanes = jnp.zeros((256, 128), jnp.float32)
-    for j in range(COLS):
-        share_lanes = jnp.where(lanes == j, share(j), share_lanes)
+
+    def scores(*pieces):
+        def product(kind, a0, na, j):
+            buf = rows_buf[kind]
+            score_buf[kind][pl.ds(a0 * 256, na * 256), pl.ds(j * 256, 256)] = lax.dot_general(
+                buf[pl.ds(a0 * 256, na * 256), :],
+                buf[pl.ds(pl.multiple_of((col_base + j) * 256, 256), 256), :],
+                pair_dims, preferred_element_type=jnp.float32,
+            ) * (logit_scale * log2e)
+            if a0 <= 3 < a0 + na and j == 0:
+                @pl.when(core == 0)
+                def _():
+                    tile = score_buf[kind][pl.ds(768, 256), pl.ds(0, 256)]
+                    row = lax.broadcasted_iota(jnp.int32, (256, 256), 0)
+                    col = lax.broadcasted_iota(jnp.int32, (256, 256), 1)
+                    score_buf[kind][pl.ds(768, 256), pl.ds(0, 256)] = jnp.where(row == col, NEG, tile)
+
+        def totals(kind, a0, na, j):
+            cols = pl.ds(j * 256, 256)
+            for a in range(a0, a0 + na):
+                for i in range(4):
+                    rows = pl.ds(a * 256 + i * 64, 64)
+                    first = score_buf[kind][rows, pl.ds(j * 256, 128)]
+                    second = score_buf[kind][rows, pl.ds(j * 256 + 128, 128)]
+                    before = top_parts[kind, rows, :]
+                    top = jnp.maximum(before, jnp.maximum(first, second))
+                    total = jnp.exp2(first - top) + jnp.exp2(second - top)
+                    sum_parts[kind, rows, :] = sum_parts[kind, rows, :] * jnp.exp2(before - top) + total * shares[j]
+                    top_parts[kind, rows, :] = top
+                tile = score_buf[kind][pl.ds(a * 256, 256), cols]
+                top = jnp.max(tile, axis=0, keepdims=True)
+                total = jnp.sum(jnp.exp2(tile - top), axis=0, keepdims=True)
+                col_top[kind, a:a + 1, cols] = top
+                col_sum[kind, a:a + 1, cols] = total
+
+        product(*pieces[0])
+        for last, piece in zip(pieces, pieces[1:]):
+            totals(*last)
+            product(*piece)
+        totals(*pieces[-1])
+
+    def arrivals(*names):
+        for name in names:
+            arrive("TUSV".index(name[0]), int(name[1:]))
+
+    arrivals("S3", "V4", "V10", "V9", "T3", "T10", "S4", "T9", "S1", "S2", "V3", "S10", "T4", "S9", "T1", "T2", "U3", "U10", "U4", "U9", "V1", "V2")
+    side_wait(S, 1, 2, 3, 4, 8, 9)
+    scores((S, 1, 3, 0), (S, 1, 3, 1))
+    arrivals("V5", "V6", "S0", "U2", "T5", "S6", "S11", "V11", "T11")
+    side_wait(S, 6, 11)
+    scores((S, 1, 3, 3))
+    arrivals("U1", "T0", "S5", "U5", "T6", "U6", "U11")
+    side_wait(T, 1, 2, 3, 4, 8, 9)
+    side_wait(S, 5, 10)
+    scores((T, 1, 3, 0), (T, 1, 3, 1), (S, 1, 3, 2))
+    arrivals("V0", "U0", "S7", "S12", "V12", "V7")
+    side_wait(T, 5, 6, 10, 11)
+    side_wait(S, 0)
+    scores((T, 1, 3, 2), (T, 1, 3, 3), *((S, 0, 1, j) for j in range(4)))
+    arrivals("T12", "U12", "T7", "U7")
+    side_wait(T, 0)
+    side_wait(S, 7, 12)
+    scores(*((T, 0, 1, j) for j in range(4)), (S, 0, 4, 4))
+    side_wait(T, 7, 12)
+    scores((T, 0, 4, 4))
 
     for a in range(4):
         rows = pl.ds(a * 256, 256)
@@ -225,9 +244,7 @@
         for kind in (T, S):
             parts = top_parts[kind, rows, :]
             top = jnp.max(parts, axis=1, keepdims=True)
-            total = jnp.sum(
-                sum_parts[kind, rows, :] * share_lanes * jnp.exp2(parts - top), axis=1, keepdims=True
-            )
+            total = jnp.sum(sum_parts[kind, rows, :] * jnp.exp2(parts - top), axis=1, keepdims=True)
             packed = jnp.where(lanes == 2 * kind, top, packed)
             packed = jnp.where(lanes == 2 * kind + 1, total, packed)
         turned = packed.T
@@ -240,7 +257,7 @@
             parts = col_top[kind, :, cols]
             top = jnp.max(parts, axis=0, keepdims=True)
             total = jnp.sum(col_sum[kind, :, cols] * jnp.exp2(parts - top), axis=0, keepdims=True)
-            lines += [top, total * share(j)]
+            lines += [top, total * shares[j]]
         lines.append(jnp.zeros((4, 256), jnp.float32))
         lines = jnp.concatenate(lines, axis=0)
         stat_out[4 + j, 0] = lines[:, 0:128]
@@ -437,41 +454,22 @@
             pl.when(core == 0)(lambda: send(0))
             pl.when(core == 1)(lambda: send(1))
 
-    weights(0)
-    for a in range(4):
-        rows_term(a)
-        if a < 3:
-            weights(a + 1)
-        part_a_copy(a).start()
-        if a == 2:
-            slot_ready(0)
-            send_sum(0, 0, 1)
-            slot_ready(1)
-            send_sum(1, 1)
-        if a == 3:
-            slot_ready(2)
-            send_sum(2, 0)
-    columns_term(4)
-    columns_term(3)
-    for slot in (7, 12):
-        slot_ready(slot)
-        send_sum(slot, 0, 1)
-    send_sum(1, 0)
-    send_sum(2, 1)
-    columns_term(2)
-    for slot in (6, 11):
-        slot_ready(slot)
-    send_sum(6, 0, 1)
-    columns_term(1)
-    for slot in (5, 10):
-        slot_ready(slot)
-    send_sum(5, 0, 1)
-    columns_term(0)
-    for slot in (4, 9, 3, 8):
-        slot_ready(slot)
-    for piece in (0, 1):
-        for slot in (11, 10, 4, 9, 3):
+    ready = set()
+    for name in ORDER:
+        if name[0] == "W":
+            weights(int(name[1:]))
+        elif name[0] == "A":
+            rows_term(int(name[1:]))
+            part_a_copy(int(name[1:])).start()
+        elif name[0] == "B":
+            columns_term(int(name[1:]))
+        else:
+            slot, piece = (int(n) for n in name.split("."))
+            if slot not in ready:
+                ready.add(slot)
+                slot_ready(slot)
             send_sum(slot, piece)
+    slot_ready(OWN)
 
     grad = logit_scale * jnp.concatenate(
         [added(slot_terms(0, OWN, piece), piece) for piece in (0, 1)], axis=0
@@ -481,7 +479,7 @@
     d_student = ((grad - student * along) / norm[:, 0:1]).astype(jnp.bfloat16)
     out[...] = lax.dot_general(d_student, proj[...], pair_dims, preferred_element_type=jnp.float32)
 
-    for kind in (T, S):
+    for kind in range(4):
         for slot in range(SLOTS):
             if slot != OWN:
                 row_copy(kind, OWN, slot).wait_send()
@@ -516,9 +514,12 @@
     return pl.pallas_call(
         kernel,
         out_shape=jax.ShapeDtypeStruct((128, 1024), f32),
-        in_specs=[vmem] * 3,
+        in_specs=[pl.BlockSpec(memory_space=pl.ANY)] * 3,
         out_specs=vmem,
         scratch_shapes=[
+            pltpu.VMEM((128, 1024), bf16),
+            pltpu.VMEM((128, 1024), bf16),
+            pltpu.VMEM((1024, 1024), bf16),
             pltpu.VMEM((SLOTS * 256, 1024), bf16),
             pltpu.VMEM((SLOTS * 256, 1024), bf16),
             pltpu.VMEM((1024, COLS * 256), f32),
@@ -539,9 +540,9 @@
             pltpu.VMEM((SLOTS, 128, 1024), bf16),
             pltpu.VMEM((128, 1024), f32),
             pltpu.VMEM((128, 128), f32),
-            dma((2, SLOTS)), dma((2, SLOTS)), dma((2, SLOTS)), dma((2, SLOTS)),
+            dma((4, SLOTS)), dma((4, SLOTS)), dma((4, SLOTS)), dma((4, SLOTS)),
             dma((18,)), dma((18,)), dma((18,)), dma((18,)),
-            dma((4,)), dma((4,)), dma((COLS,)), dma((COLS,)), dma((2 * SLOTS,)), dma((2 * SLOTS,)),
+            dma((4,)), dma((4,)), dma((COLS,)), dma((COLS,)), dma((2 * SLOTS,)), dma((2 * SLOTS,)), dma((3,)),
         ],
         compiler_params=pltpu.CompilerParams(
             collective_id=0, has_side_effects=True, vmem_limit_bytes=60 * 2**20

time: 98.3 us -> 85.5 us (0.87)
  Pallas kernels: 95.2 us -> 82.4 us
    pallas_call x1, Pallas kernels: 95.2 us -> 82.4 us  [per_device(): pl.pallas_call(kernel, out_shape=jax.ShapeDtypeStruct((128, 1024), f32),...]
where the time goes in v3:
time: 85.5 us; the launch traced here: 84.3 us
  Pallas kernels  82.4 us (96%)
  local copies, waits for them, and re-layouts  1.89 us (2%)
    pallas_call x1, Pallas kernels, per_device(): pl.pallas_call(kernel, out_shape=jax.ShapeDtypeStruct((128, 1024), f32),...  82.4 us
    unnamed x1, local copies, waits for them, and re-layouts  1.89 us

profile of v3, /device:TPU:0, one launch (start us, length us, event | category | flops | bytes accessed | tf_op | source)
XLA Modules:
  0.0 84.3 jit_solution(16047177393690240634)
XLA Ops:
  0.0 82.4 %shard_map.37 = f32[128,1024]{1,0:T(8,128)} custom-call(bf16[128,1024]{1,0:T(8,128)(2,1)} %features_in.1, bf16[128,1024]{1,0:T(8,128)(2,1)} %teacher_in.1, bf16[1024,1024]{1,0:T(8,128)(2,1)} %proj_in.1), custom_call_target="tpu_custom_call" | custom-call | flops 8999999488 | bytes 4000000 | tf_op jit(solution)/shard_map/pallas_call | solution.py:514
  82.4 1.9 %copy.5 = f32[128,1024]{1,0:T(8,128)} copy(f32[128,1024]{1,0:T(8,128)} %shard_map.37) | data formatting | bytes 1048576

commit v4 on v3

--- a/solution.py
+++ b/solution.py
@@ -1,4 +1,5 @@
 import functools
+import itertools
 
 import jax
 import jax.numpy as jnp
@@ -22,13 +23,19 @@
 COLS = 5
 SHARE = ((0.5, 1.0, 1.0, 1.0, 0.5), (1.0, 1.0, 0.5, 1.0, 0.5))
 FROM = (
-    ((2, 3, 3, 8, 8, 9, 4, 5, -1, 8, 8, 4, 6), (2, 3, 3, 8, 8, 9, 10, 11, -1, 8, 8, 9, 6)),
-    ((2, 3, 3, 8, 8, 9, 10, 11, -1, 8, 8, 9, 11), (2, 3, 3, 8, 8, 3, 4, 5, -1, 8, 8, 9, 11)),
-    ((1, 3, 3, 8, 8, 3, 4, 11, -1, 8, 8, 4, 11), (1, 3, 3, 8, 8, 9, 4, 11, -1, 8, 8, 4, 11)),
-    ((1, 3, 3, 8, 8, 9, 4, 5, -1, 8, 8, 9, 6), (1, 3, 3, 8, 8, 9, 4, 5, -1, 8, 8, 4, 6)),
+    ((2, 3, 3, 8, 8, 9, 4, 5, -1, 8, 8, 9, 6), (1, 3, 3, 8, 8, 9, 4, 11, -1, 8, 8, 9, 6)),
+    ((1, 3, 3, 8, 8, 3, 4, 11, -1, 8, 8, 4, 6), (2, 3, 3, 8, 8, 9, 4, 11, -1, 8, 8, 4, 11)),
+    ((2, 3, 3, 8, 8, 9, 4, 5, -1, 8, 8, 4, 6), (2, 3, 3, 8, 8, 9, 4, 11, -1, 8, 8, 4, 11)),
+    ((1, 3, 3, 8, 8, 3, 10, 5, -1, 8, 8, 9, 6), (1, 3, 3, 8, 8, 9, 4, 11, -1, 8, 8, 9, 11)),
 )
 FIRST = (
-    "S3", "V10", "V4", "V9", "S4", "T3", "T4", "T9", "U4", "V3", "S9", "T10", "U3", "S10", "U10", "U9",
+    "S3", "U10", "V9", "V10", "T9", "S9", "T10", "V3", "U4", "S4", "S10", "U9", "U3", "T4", "V4", "T3",
+)
+STEPS = (
+    "S3", "U10", "U4", "V3", "T9", "V10", "U3", "V9", "T3", "T4", "S4", "S9", "V2", "S10", "S2", "V1", "S1", "U2",
+    "T5", "V5", "U1", "U9", "V4", "s0", "U11", "U6", "s1", "T2", "V11", "T1", "S5", "V6", "T10", "T6", "T11", "s2",
+    "t1", "t0", "S11", "S0", "V0", "S6", "U5", "t3", "U0", "U7", "T0", "s7", "t2", "s3", "t5", "s6", "s4", "t7",
+    "t6", "V7", "U12", "S7", "V12", "S12", "T7", "T12", "s5", "t8", "s8", "t4",
 )
 INTO = (
     ((2, 3, 3, 8, 8, 9, 4, 5, -1, 8, 8, 9, 10), (2, 3, 3, 8, 8, 9, 4, 11, -1, 8, 8, 4, 11)),
@@ -58,7 +65,7 @@
     s_rows, t_rows, s_score, t_score, weight, top_parts, sum_parts, col_top, col_sum,
     stat_out, stat_in, lse_out, lse_in, lse_rows, part_a, part_b, stage, joined,
     unit, norm,
-    g_send, g_recv, c_send, c_recv, st_send, st_recv, l_send, l_recv,
+    g_send, g_recv, c_send, st_send, st_recv, l_send, l_recv,
     pa_send, pa_recv, pb_send, pb_recv, r_send, r_recv, in_sem,
 ):
     loads = [
@@ -82,7 +89,8 @@
 
     barrier = pltpu.get_barrier_semaphore()
     for move in NEIGHBOURS:
-        pl.semaphore_signal(barrier, inc=1, device_id=device(move, core), device_id_type=MESH)
+        for to_core in (0, 1):
+            pl.semaphore_signal(barrier, inc=1, device_id=device(move, to_core), device_id_type=MESH)
     pl.semaphore_signal(barrier, inc=1, device_id=sibling, device_id_type=MESH)
 
     def remote(src, dst, send, recv, target):
@@ -93,22 +101,32 @@
     def piece_rows(q, slot, which):
         return rows_buf[q // 2].at[pl.ds(slot * 256 + which + (q % 2) * 64, 64)]
 
+    def user(slot):
+        return 0 if slot < OWN else 1
+
+    def straight(q, slot):
+        return slot >= 4 and slot != OWN and slot not in FROM[q][1 - user(slot)]
+
     def row_copy(q, src_slot, slot):
         move = step(PLACE[src_slot], PLACE[slot])
+        to_core, crossed = core, 0
+        if straight(q, slot):
+            to_core = user(slot)
+            crossed = jnp.where(core == to_core, 0, 1)
         return remote(
             piece_rows(q, src_slot, half), piece_rows(q, slot, half),
-            g_send.at[q, slot], g_recv.at[q, slot], device(move, core),
+            g_send.at[q, slot], g_recv.at[crossed, q, slot], device(move, to_core),
         )
 
     def side_copy(q, slot, which):
         piece = piece_rows(q, slot, which)
-        return remote(piece, piece, c_send.at[q, slot], c_recv.at[q, slot], sibling)
+        return remote(piece, piece, c_send.at[q, slot], g_recv.at[1, q, slot], sibling)
 
     def to_side(q, slot):
         if slot < 4:
             side_copy(q, slot, half).start()
-        else:
-            @pl.when(core == (1 if slot < OWN else 0))
+        elif not straight(q, slot):
+            @pl.when(core != user(slot))
             def _():
                 side_copy(q, slot, half).start()
 
@@ -117,8 +135,14 @@
             row_copy(q, slot, child).start()
 
     def arrive(q, slot):
+        children = [[d for d in range(SLOTS) if FROM[q][which][d] == slot] for which in (0, 1)]
+        if straight(q, slot):
+            @pl.when(core == user(slot))
+            def _():
+                row_copy(q, OWN, slot).wait_recv()
+                start_rows(q, slot, children[user(slot)])
+            return
         row_copy(q, OWN, slot).wait_recv()
-        children = [[d for d in range(SLOTS) if FROM[q][which][d] == slot] for which in (0, 1)]
         if children[0] == children[1]:
             start_rows(q, slot, children[0])
         else:
@@ -133,7 +157,7 @@
                 if slot < 4:
                     side_copy(q, slot, 128 - half).wait_recv()
                 else:
-                    @pl.when(core == (0 if slot < OWN else 1))
+                    @pl.when(core == user(slot))
                     def _(slot=slot, q=q):
                         side_copy(q, slot, 128 - half).wait_recv()
 
@@ -152,7 +176,7 @@
     norm[...] = jnp.broadcast_to(length, norm.shape)
     s_rows[own_rows, :] = student.astype(jnp.bfloat16)
 
-    pl.semaphore_wait(barrier, len(NEIGHBOURS) + 1)
+    pl.semaphore_wait(barrier, 2 * len(NEIGHBOURS) + 1)
     for name in FIRST:
         start_rows("TUSV".index(name[0]), OWN, (int(name[1:]),))
     for q in range(4):
@@ -213,32 +237,28 @@
             product(*piece)
         totals(*pieces[-1])
 
-    def arrivals(*names):
+    waited = set()
+
+    def tiles(names):
+        pieces = []
         for name in names:
-            arrive("TUSV".index(name[0]), int(name[1:]))
-
-    arrivals("S3", "V4", "V10", "V9", "T3", "T10", "S4", "T9", "S1", "S2", "V3", "S10", "T4", "S9", "T1", "T2", "U3", "U10", "U4", "U9", "V1", "V2")
-    side_wait(S, 1, 2, 3, 4, 8, 9)
-    scores((S, 1, 3, 0), (S, 1, 3, 1))
-    arrivals("V5", "V6", "S0", "U2", "T5", "S6", "S11", "V11", "T11")
-    side_wait(S, 6, 11)
-    scores((S, 1, 3, 3))
-    arrivals("U1", "T0", "S5", "U5", "T6", "U6", "U11")
-    side_wait(T, 1, 2, 3, 4, 8, 9)
-    side_wait(S, 5, 10)
-    scores((T, 1, 3, 0), (T, 1, 3, 1), (S, 1, 3, 2))
-    arrivals("V0", "U0", "S7", "S12", "V12", "V7")
-    side_wait(T, 5, 6, 10, 11)
-    side_wait(S, 0)
-    scores((T, 1, 3, 2), (T, 1, 3, 3), *((S, 0, 1, j) for j in range(4)))
-    arrivals("T12", "U12", "T7", "U7")
-    side_wait(T, 0)
-    side_wait(S, 7, 12)
-    scores(*((T, 0, 1, j) for j in range(4)), (S, 0, 4, 4))
-    side_wait(T, 7, 12)
-    scores((T, 0, 4, 4))
-
-    for a in range(4):
+            kind, n = "ts".index(name[0]), int(name[1:])
+            a0, na, j = (1, 3, n) if n < 4 else (0, 1, n - 4) if n < 8 else (0, 4, 4)
+            for slot in (*range(a0, a0 + na), 3 + j, 8 + j):
+                if (kind, slot) not in waited:
+                    waited.add((kind, slot))
+                    side_wait(kind, slot)
+            pieces.append((kind, a0, na, j))
+        scores(*pieces)
+
+    for upper, names in itertools.groupby(STEPS, str.isupper):
+        if upper:
+            for name in names:
+                arrive("TUSV".index(name[0]), int(name[1:]))
+        else:
+            tiles(list(names))
+
+    def row_totals(a):
         rows = pl.ds(a * 256, 256)
         packed = jnp.zeros((256, 128), jnp.float32)
         for kind in (T, S):
@@ -250,7 +270,7 @@
         turned = packed.T
         stat_out[a, 0] = turned[0:8, 0:128]
         stat_out[a, 1] = turned[0:8, 128:256]
-    for j in range(COLS):
+    def column_totals(j):
         cols = pl.ds(j * 256, 256)
         lines = []
         for kind in (T, S):
@@ -290,7 +310,11 @@
     def keep_stat():
         stat_in[9 + 4] = stat_out[4, 1]
 
-    for index in range(9):
+    for index in (8, 7, 0, 1, 2, 6, 5, 3, 4):
+        if index < 4:
+            row_totals(index)
+        else:
+            column_totals(index - 4)
         for to_half in (0, 1):
             unless_own(index, to_half, lambda: stat_copy(index, to_half).start(), keep_stat)
 
@@ -329,7 +353,7 @@
     def keep_lse():
         lse_in[4, 1] = lse_out[...]
 
-    for index in range(9):
+    for index in (8, 0, 7, 1, 2, 6, 5, 3, 4):
         for of_core in (0, 1):
             if index == 4 and of_core == 1:
                 pl.when(core == 0)(lambda: lse_copy(1, 4).start())
@@ -485,8 +509,8 @@
                 row_copy(kind, OWN, slot).wait_send()
             if slot < 4:
                 side_copy(kind, slot, half).wait_send()
-            else:
-                @pl.when(core == (1 if slot < OWN else 0))
+            elif not straight(kind, slot):
+                @pl.when(core != user(slot))
                 def _(kind=kind, slot=slot):
                     side_copy(kind, slot, half).wait_send()
     for index in range(9):
@@ -540,7 +564,7 @@
             pltpu.VMEM((SLOTS, 128, 1024), bf16),
             pltpu.VMEM((128, 1024), f32),
             pltpu.VMEM((128, 128), f32),
-            dma((4, SLOTS)), dma((4, SLOTS)), dma((4, SLOTS)), dma((4, SLOTS)),
+            dma((4, SLOTS)), dma((2, 4, SLOTS)), dma((4, SLOTS)),
             dma((18,)), dma((18,)), dma((18,)), dma((18,)),
             dma((4,)), dma((4,)), dma((COLS,)), dma((COLS,)), dma((2 * SLOTS,)), dma((2 * SLOTS,)), dma((3,)),
         ],

time: 85.5 us -> 79.5 us (0.930)
  Pallas kernels: 82.4 us -> 76.4 us
    pallas_call x1, Pallas kernels: 82.4 us -> 76.4 us  [per_device(): pl.pallas_call(kernel, out_shape=jax.ShapeDtypeStruct((128, 1024), f32),...]
where the time goes in v4:
time: 79.5 us; the launch traced here: 78.3 us
  Pallas kernels  76.4 us (96%)
  local copies, waits for them, and re-layouts  1.89 us (2%)
    pallas_call x1, Pallas kernels, per_device(): pl.pallas_call(kernel, out_shape=jax.ShapeDtypeStruct((128, 1024), f32),...  76.4 us
    unnamed x1, local copies, waits for them, and re-layouts  1.89 us

profile of v4, /device:TPU:0, one launch (start us, length us, event | category | flops | bytes accessed | tf_op | source)
XLA Modules:
  0.0 78.3 jit_solution(11332253388133586820)
XLA Ops:
  0.0 76.4 %shard_map.37 = f32[128,1024]{1,0:T(8,128)} custom-call(bf16[128,1024]{1,0:T(8,128)(2,1)} %features_in.1, bf16[128,1024]{1,0:T(8,128)(2,1)} %teacher_in.1, bf16[1024,1024]{1,0:T(8,128)(2,1)} %proj_in.1), custom_call_target="tpu_custom_call" | custom-call | flops 8999999488 | bytes 4000000 | tf_op jit(solution)/shard_map/pallas_call | solution.py:538
  76.4 1.9 %copy.5 = f32[128,1024]{1,0:T(8,128)} copy(f32[128,1024]{1,0:T(8,128)} %shard_map.37) | data formatting | bytes 1048576

commit v5 on v4

--- a/solution.py
+++ b/solution.py
@@ -38,12 +38,13 @@
     "t6", "V7", "U12", "S7", "V12", "S12", "T7", "T12", "s5", "t8", "s8", "t4",
 )
 INTO = (
-    ((2, 3, 3, 8, 8, 9, 4, 5, -1, 8, 8, 9, 10), (2, 3, 3, 8, 8, 9, 4, 11, -1, 8, 8, 4, 11)),
-    ((1, 3, 3, 8, 8, 9, 4, 5, -1, 8, 8, 9, 10), (1, 3, 3, 8, 8, 9, 4, 11, -1, 8, 8, 4, 6)),
+    ((1, 3, 3, 8, 8, 9, 4, 5, -1, 8, 8, 9, 11), (1, 3, 3, 8, 8, 9, 4, 11, -1, 8, 8, 4, 10)),
+    ((3, 3, 3, 8, 8, 9, 10, 5, -1, 8, 8, 9, 10), (1, 3, 3, 8, 8, 9, 4, 11, -1, 8, 8, 4, 11)),
 )
 ORDER = (
-    "W0", "A0", "W1", "W2", "W3", "B4", "0.0", "A1", "7.0", "7.1", "0.1", "12.1", "A2", "B2", "12.0", "B3",
-    "5.1", "6.0", "1.0", "2.0", "B1", "A3", "5.0", "1.1", "11.0", "11.1", "6.1", "B0", "2.1", "10.1", "4.0", "9.1", "3.0", "10.0", "9.0", "3.1", "4.1",
+    "W0", "A0", "W1", "W2", "W3", "B4", "0.0", "A2", "7.1", "7.0", "0.1", "12.0", "12.1", "A1", "B2", "B3", "2.0", "5.1",
+    "6.0", "2.1", "1.0", "B1", "6.1", "A3", "5.0", "11.1", "11.0", "B0", "1.1", "10.0", "9.1", "3.0", "4.0", "4.1", "10.1", "9.0",
+    "3.1",
 )
 T, S = 0, 1
 
@@ -89,8 +90,7 @@
 
     barrier = pltpu.get_barrier_semaphore()
     for move in NEIGHBOURS:
-        for to_core in (0, 1):
-            pl.semaphore_signal(barrier, inc=1, device_id=device(move, to_core), device_id_type=MESH)
+        pl.semaphore_signal(barrier, inc=1, device_id=device(move, core), device_id_type=MESH)
     pl.semaphore_signal(barrier, inc=1, device_id=sibling, device_id_type=MESH)
 
     def remote(src, dst, send, recv, target):
@@ -105,7 +105,8 @@
         return 0 if slot < OWN else 1
 
     def straight(q, slot):
-        return slot >= 4 and slot != OWN and slot not in FROM[q][1 - user(slot)]
+        source = FROM[q][1 - user(slot)]
+        return slot >= 4 and slot != OWN and source[slot] != OWN and slot not in source
 
     def row_copy(q, src_slot, slot):
         move = step(PLACE[src_slot], PLACE[slot])
@@ -176,7 +177,7 @@
     norm[...] = jnp.broadcast_to(length, norm.shape)
     s_rows[own_rows, :] = student.astype(jnp.bfloat16)
 
-    pl.semaphore_wait(barrier, 2 * len(NEIGHBOURS) + 1)
+    pl.semaphore_wait(barrier, len(NEIGHBOURS) + 1)
     for name in FIRST:
         start_rows("TUSV".index(name[0]), OWN, (int(name[1:]),))
     for q in range(4):
@@ -479,12 +480,15 @@
             pl.when(core == 1)(lambda: send(1))
 
     ready = set()
-    for name in ORDER:
+    for at, name in enumerate(ORDER):
         if name[0] == "W":
             weights(int(name[1:]))
+            if ORDER[at - 1][0] == "A":
+                part_a_copy(int(ORDER[at - 1][1:])).start()
         elif name[0] == "A":
             rows_term(int(name[1:]))
-            part_a_copy(int(name[1:])).start()
+            if ORDER[at + 1][0] != "W":
+                part_a_copy(int(name[1:])).start()
         elif name[0] == "B":
             columns_term(int(name[1:]))
         else:
@@ -495,13 +499,12 @@
             send_sum(slot, piece)
     slot_ready(OWN)
 
-    grad = logit_scale * jnp.concatenate(
-        [added(slot_terms(0, OWN, piece), piece) for piece in (0, 1)], axis=0
-    )
-    student = unit[...]
-    along = jnp.sum(student * grad, axis=1, keepdims=True)
-    d_student = ((grad - student * along) / norm[:, 0:1]).astype(jnp.bfloat16)
-    out[...] = lax.dot_general(d_student, proj[...], pair_dims, preferred_element_type=jnp.float32)
+    for piece in (0, 1):
+        rows = pl.ds(piece * 64, 64)
+        grad = logit_scale * added(slot_terms(0, OWN, piece), piece)
+        student = unit[rows, :]
+        along = jnp.sum(student * grad, axis=1, keepdims=True)
+        out[rows, :] = ((grad - student * along) / norm[rows, 0:1]).astype(jnp.bfloat16)
 
     for kind in range(4):
         for slot in range(SLOTS):
@@ -535,9 +538,9 @@
     bf16, f32 = jnp.bfloat16, jnp.float32
     vmem = pl.BlockSpec(memory_space=pltpu.VMEM)
     dma = pltpu.SemaphoreType.DMA
-    return pl.pallas_call(
+    d_student = pl.pallas_call(
         kernel,
-        out_shape=jax.ShapeDtypeStruct((128, 1024), f32),
+        out_shape=jax.ShapeDtypeStruct((128, 1024), bf16),
         in_specs=[pl.BlockSpec(memory_space=pl.ANY)] * 3,
         out_specs=vmem,
         scratch_shapes=[
@@ -573,6 +576,9 @@
         ),
         cost_estimate=pl.CostEstimate(flops=9_000_000_000, bytes_accessed=4_000_000, transcendentals=9_000_000),
     )(features, teacher, proj)
+    return lax.dot_general(
+        d_student, proj, (((1,), (1,)), ((), ())), preferred_element_type=f32
+    )
 
 
 def solution(mesh):

time: 79.5 us -> 79.2 us (level)
  matrix products: 0 us -> 2.57 us
  local copies, waits for them, and re-layouts: 1.89 us -> 0.01 us
    dot_general x0 -> x1, matrix products: none -> 2.57 us  [per_device(): lax.dot_general(d_student, proj, (((1,), (1,)), ((), ())), preferred_elem...]
    unnamed x1 -> x2, local copies, waits for them, and re-layouts: 1.89 us -> 0.01 us
where the time goes in v5:
time: 79.2 us; the launch traced here: 78.3 us
  Pallas kernels  75.7 us (96%)
  matrix products  2.57 us (3%)
    pallas_call x1, Pallas kernels, per_device(): pl.pallas_call(kernel, out_shape=jax.ShapeDtypeStruct((128, 1024), bf16),...  75.7 us
    dot_general x1, matrix products, per_device(): lax.dot_general(d_student, proj, (((1,), (1,)), ((), ())), preferred_elem...  2.57 us

profile of v5, /device:TPU:0, one launch (start us, length us, event | category | flops | bytes accessed | tf_op | source)
XLA Modules:
  0.0 78.3 jit_solution(10347555986107221615)
XLA Ops:
  0.0 0.0 copy-start
  0.0 75.7 %shard_map.37 = bf16[128,1024]{1,0:T(8,128)(2,1)} custom-call(bf16[128,1024]{1,0:T(8,128)(2,1)} %features_in.1, bf16[128,1024]{1,0:T(8,128)(2,1)} %teacher_in.1, bf16[1024,1024]{1,0:T(8,128)(2,1)} %proj_in.1), custom_call_target="tpu_custom_call" | custom-call | flops 8999999488 | bytes 4000000 | tf_op jit(solution)/shard_map/pallas_call | solution.py:541
  75.7 0.0 copy-done
  75.7 2.6 %fusion = f32[128,1024]{1,0:T(8,128)} fusion(bf16[128,1024]{1,0:T(8,128)(2,1)} %shard_map.37, bf16[1024,1024]{1,0:T(8,128)(2,1)S(1)} %copy-done), kind=kOutput, calls=%fused_computation | convolution fusion | flops 268435456 | bytes 2883584 | tf_op jit(solution)/shard_map/dot_general | solution.py:579
Async XLA Ops:
  0.0 75.7 %copy-start = (bf16[1024,1024]{1,0:T(8,128)(2,1)S(1)}, bf16[1024,1024]{1,0:T(8,128)(2,1)}, u32[]{:S(2)}) copy-start(bf16[1024,1024]{1,0:T(8,128)(2,1)} %proj_in.1) | copy-start | bytes 6291460

commit v6 on v5

--- a/solution.py
+++ b/solution.py
@@ -361,6 +361,14 @@
                 pl.when(core == 1)(keep_lse)
             else:
                 lse_copy(of_core, index).start()
+    def roots(i, carry):
+        rows = pl.ds(pl.multiple_of(i * 64, 64), 64)
+        for score in score_buf:
+            score[rows, :] = jnp.exp2(score[rows, :] * 0.5)
+        return carry
+
+    lax.fori_loop(0, 16, roots, 0)
+
     for index in range(9):
         for from_half in (0, 1):
             unless_own(index, from_half, lambda: lse_arrival(index, from_half).wait_recv())
@@ -368,7 +376,7 @@
     for a in range(4):
         lines = jnp.concatenate(
             [
-                jnp.concatenate([lse_in[a, 0], lse_in[a, 1]], axis=1),
+                jnp.exp2(-0.5 * jnp.concatenate([lse_in[a, 0], lse_in[a, 1]], axis=1)),
                 jnp.zeros((120, 256), jnp.float32),
             ],
             axis=0,
@@ -376,18 +384,20 @@
         for kind in (T, S):
             lse_rows[kind, pl.ds(a * 256, 256), :] = jnp.broadcast_to(lines[:, kind:kind + 1], (256, 128))
 
+    def square(value):
+        return value * value
+
     def weights(a):
         for j in range(COLS):
             for side in (0, 1):
+                col_roots = [jnp.exp2(-0.5 * lse_in[4 + j, side, kind:kind + 1, :]) for kind in (T, S)]
                 for i in range(4):
                     rows = pl.ds(a * 256 + i * 64, 64)
                     cols = pl.ds(j * 256 + side * 128, 128)
                     s_tile, t_tile = s_score[rows, cols], t_score[rows, cols]
                     value = (
-                        jnp.exp2(s_tile - lse_rows[S, rows, :])
-                        + jnp.exp2(s_tile - lse_in[4 + j, side, S:S + 1, :])
-                        - jnp.exp2(t_tile - lse_rows[T, rows, :])
-                        - jnp.exp2(t_tile - lse_in[4 + j, side, T:T + 1, :])
+                        square(s_tile * lse_rows[S, rows, :]) + square(s_tile * col_roots[S])
+                        - square(t_tile * lse_rows[T, rows, :]) - square(t_tile * col_roots[T])
                     )
                     weight[rows, cols] = (value * shares[j]).astype(jnp.bfloat16)
 

time: 79.2 us -> 78.6 us (level)
  no operation moved by 1% of the time
where the time goes in v6:
time: 78.6 us; the launch traced here: 77.7 us
  Pallas kernels  75.1 us (96%)
  matrix products  2.57 us (3%)
    pallas_call x1, Pallas kernels, per_device(): pl.pallas_call(kernel, out_shape=jax.ShapeDtypeStruct((128, 1024), bf16),...  75.1 us
    dot_general x1, matrix products, per_device(): lax.dot_general(d_student, proj, (((1,), (1,)), ((), ())), preferred_elem...  2.57 us

profile of v6, /device:TPU:0, one launch (start us, length us, event | category | flops | bytes accessed | tf_op | source)
XLA Modules:
  0.0 77.7 jit_solution(281501273720200483)
XLA Ops:
  0.0 0.0 copy-start
  0.0 75.1 %shard_map.37 = bf16[128,1024]{1,0:T(8,128)(2,1)} custom-call(bf16[128,1024]{1,0:T(8,128)(2,1)} %features_in.1, bf16[128,1024]{1,0:T(8,128)(2,1)} %teacher_in.1, bf16[1024,1024]{1,0:T(8,128)(2,1)} %proj_in.1), custom_call_target="tpu_custom_call" | custom-call | flops 8999999488 | bytes 4000000 | tf_op jit(solution)/shard_map/pallas_call | solution.py:551
  75.1 0.0 copy-done
  75.1 2.6 %fusion = f32[128,1024]{1,0:T(8,128)} fusion(bf16[128,1024]{1,0:T(8,128)(2,1)} %shard_map.37, bf16[1024,1024]{1,0:T(8,128)(2,1)S(1)} %copy-done), kind=kOutput, calls=%fused_computation | convolution fusion | flops 268435456 | bytes 2883584 | tf_op jit(solution)/shard_map/dot_general | solution.py:589
Async XLA Ops:
  0.0 75.1 %copy-start = (bf16[1024,1024]{1,0:T(8,128)(2,1)S(1)}, bf16[1024,1024]{1,0:T(8,128)(2,1)}, u32[]{:S(2)}) copy-start(bf16[1024,1024]{1,0:T(8,128)(2,1)} %proj_in.1) | copy-start | bytes 6291460
